TPU v7x, 32 devices: a whole 2x2x4 slice. The times are simulated.
32 devices in a mesh: rep: 2 (over y), grp: 8 (over z, x), tp: 2 (over core).
Axes of the slice: x: 2, y: 2, z: 4, core: 2. Of those that a mesh axis runs over, the one named last changes fastest.
Arguments:
- counts: int32 [16], P(('rep', 'grp')), parts along dimension 0, may hold values from 1 to 8, as said below
- hop_offsets: int32 [128], P(('rep', 'grp')), parts along dimension 0, may hold values from -2 to 2, as said below
- write_pos: int32 [128], P(('rep', 'grp')), parts along dimension 0, may hold values from 0 to 123
- kv_cache: bfloat16 [128, 2, 128, 1024], P(('rep', 'grp'), None, None, 'tp'), parts along dimension 0, may hold values from -27 to 27
- queries: bfloat16 [128, 2, 8192], P(('rep', 'grp'), None, 'tp'), parts along dimension 0, may hold values from -6 to 6
- fresh_kv: bfloat16 [128, 2, 2, 1024], P(('rep', 'grp'), None, None, 'tp'), parts along dimension 0, may hold values from -6 to 6
Outputs:
- new_cache: bfloat16 [128, 2, 128, 1024], P(('rep', 'grp'), None, None, 'tp'), parts along dimension 0
- attended: bfloat16 [128, 2, 8192], P(('rep', 'grp'), None, 'tp'), parts along dimension 0
- served: int32 [16], P('rep'), parts along dimension 0
There are 2 independent parts, one for each index of `rep`. A program takes and returns all parts, laid end to end along the dimension named above; each array names one. Nothing has to cross between parts.
Inputs may be any that keep to these rules, and one draw needn't show every extreme that they name: `counts`: live streams fill a group's first slots; some group holds 8 streams; groups that send hold 8 streams, the others 1 or 2. `hop_offsets`: zero for empty slots and staying streams. A group sends at most one stream with each offset, and no group holds more than 8 streams after the move; offsets -2 and 2 occur.
All inputs are finite; a program needn't handle non-finite values.
Results may differ from a plain program's by a relative error of at most 0.0049.
Values may be sent and summed in bfloat16 or wider, within the bound.
No kernel may reach another device: no remote copies, remote signals or barrier semaphores. Data moves between devices by JAX's collectives and lax.ppermute only.
A program may use at most 64 MiB of HBM per device.

v0:
```python
import functools

import jax
import jax.numpy as jnp
from jax import lax
from jax.experimental import pallas as pl
from jax.experimental.pallas import tpu as pltpu
from jax.sharding import PartitionSpec as P

HEAD_DIM = 128
SINK = 4
REACH = 2
STEPS = 2
OFFSETS = tuple(o for o in range(-REACH, REACH + 1) if o != 0)
PACKS = ((-2, -1), (1, 2))
NEAR = (-1, -2)
ARRIVALS = ((-2, -1, 1), (2,))
PATCH = 16
LANES = HEAD_DIM
STAY = 0
SENT = 1
POS = SENT + len(OFFSETS)
VMEM_LIMIT = 32 * 1024 * 1024

VMEM_SPEC = pl.BlockSpec(memory_space=pltpu.VMEM)
SMEM_SPEC = pl.BlockSpec(memory_space=pltpu.SMEM)
ANY_SPEC = pl.BlockSpec(memory_space=pl.ANY)
HBM_SPEC = pl.BlockSpec(memory_space=pltpu.HBM)


def shifted(block, distance):
    count = lax.axis_size("grp")
    return lax.ppermute(block, "grp", [(i, (i + distance) % count) for i in range(count)])


def relay_shifts(groups):
    known = {0, *(-o % groups for o in NEAR)}
    late = {-o % groups for o in OFFSETS}
    shifts = []
    while len(known | late) < groups:
        best = max(range(1, groups), key=lambda d: len(known | {(k - d) % groups for k in known} | late))
        known |= {(k - best) % groups for k in known}
        shifts.append(best)
    return shifts


def load_plan(sources, targets, sem):
    copies = [pltpu.make_async_copy(a, b, sem) for a, b in zip(sources, targets)]
    for copy in copies:
        copy.start()
    for copy in copies:
        copy.wait()


def row_iota(shape):
    return lax.broadcasted_iota(jnp.int32, shape, 0)


def lane_iota(shape):
    return lax.broadcasted_iota(jnp.int32, shape, len(shape) - 1)


def head_lanes(head):
    return slice(head * HEAD_DIM, (head + 1) * HEAD_DIM)


def first_written(position, cache_len):
    return SINK + lax.rem(position, cache_len - SINK)


def plan_row(hops, live, slots, shape):
    lane = lane_iota(shape)
    stay = jnp.int32(0)
    for s in range(slots):
        stay = stay + jnp.where((s < live) & (hops[s] == 0), 1, 0)
    values = jnp.where(lane == STAY, stay, 0)
    for k, offset in enumerate(OFFSETS):
        sent = jnp.int32(0)
        for s in range(slots):
            sent = jnp.where((s < live) & (hops[s] == offset), 1, sent)
        values = jnp.where(lane == SENT + k, sent, values)
    return values


def pack_kernel(offsets, counts, hops_in, positions_in, kv, *refs):
    blocks = refs[: len(offsets)]
    hops, positions, plan_sem, sems = refs[len(offsets) :]
    load_plan((hops_in, positions_in), (hops, positions), plan_sem)
    slots, _, cache_len, _ = kv.shape
    picks, copies = [], []
    for k, offset in enumerate(offsets):
        pick = jnp.int32(0)
        for s in range(slots):
            pick = jnp.where(hops[s] == offset, s, pick)
        picks.append(pick)
        copies.append(pltpu.make_async_copy(kv.at[pick], blocks[k], sems.at[k]))
        copies[k].start()
    shape = (PATCH, LANES)
    lane, row = lane_iota(shape), row_iota(shape)
    shared = plan_row(hops, counts[0], slots, shape)
    for k in range(len(offsets)):
        position = positions[picks[k]]
        header = jnp.where(lane == POS, position, shared).astype(jnp.float32)
        first = first_written(position, cache_len)
        base = pl.multiple_of((first // PATCH) * PATCH, PATCH)
        copies[k].wait()
        top = blocks[k][0, :PATCH, :LANES].astype(jnp.float32)
        blocks[k][0, :PATCH, :LANES] = jnp.where(row == 0, header, top).astype(jnp.bfloat16)
        patch = blocks[k][0, pl.ds(base, PATCH), :LANES].astype(jnp.float32)
        patch = jnp.where(row == first - base, top[0:1], patch)
        blocks[k][0, pl.ds(base, PATCH), :LANES] = patch.astype(jnp.bfloat16)


def header_of(block):
    return block[0, :PATCH, :LANES].astype(jnp.float32).astype(jnp.int32)


def with_row(table, group, header):
    return jnp.where(row_iota(table.shape) == group, header[0:1], table)


def relay_kernel(own, *refs):
    blocks, table = refs[: len(NEAR)], refs[len(NEAR)]
    groups = table.shape[0]
    here = lax.axis_index("grp")
    rows = with_row(jnp.zeros(table.shape, jnp.int32), here, own[...])
    for offset, block in zip(NEAR, blocks):
        rows = with_row(rows, lax.rem(here - offset + groups, groups), header_of(block))
    table[...] = rows


def attend(old, new, has_header, position, queries, fresh, heads, flush):
    cache_len, width = old.shape[1:]
    head_count = width // HEAD_DIM
    group_size = queries.shape[-1] // width
    first = first_written(position, cache_len)
    second = first_written(position + 1, cache_len)
    for side in range(2):
        written = fresh[side].astype(jnp.float32)
        for head in range(head_count):
            lanes = head_lanes(head)
            rows = old[side, :, lanes].astype(jnp.float32)
            row = row_iota(rows.shape)
            if has_header and (side, head) == (0, 0):
                top = jnp.sum(jnp.where(row == first, rows, 0.0), axis=0, keepdims=True)
                rows = jnp.where(row == 0, top, rows)
            rows = jnp.where(row == second, written[1:2, lanes], jnp.where(row == first, written[0:1, lanes], rows))
            new[side, :, lanes] = rows.astype(jnp.bfloat16)
    flush()

    def both(side, head):
        return jnp.concatenate([new[side, :, head_lanes(head)], old[side, :, head_lanes(head)]], axis=0)

    scores = []
    for head in range(head_count):
        query = jnp.concatenate([queries[:, head_lanes(head * group_size + i)] for i in range(group_size)], axis=0)
        scores.append(
            lax.dot_general(query, both(0, head), (((1,), (1,)), ((), ())), preferred_element_type=jnp.float32)
        )
    scores = jnp.concatenate(scores, axis=0)
    shape = (scores.shape[0], cache_len)
    stale = (row_iota(shape) % STEPS == 0) & (lane_iota(shape) == second)
    scores = jnp.where(stale, scores[:, cache_len:], scores[:, :cache_len]) * HEAD_DIM ** (-0.5)
    weights = jnp.exp(scores - jnp.max(scores, axis=1, keepdims=True))
    weights = weights / jnp.sum(weights, axis=1, keepdims=True)
    weights = jnp.concatenate([jnp.where(stale, 0.0, weights), jnp.where(stale, weights, 0.0)], axis=1)
    weights = weights.astype(jnp.bfloat16)
    for head in range(head_count):
        rows = slice(head * group_size * STEPS, (head + 1) * group_size * STEPS)
        mixed = jnp.dot(weights[rows], both(1, head), preferred_element_type=jnp.float32).astype(jnp.bfloat16)
        for i in range(group_size):
            heads[:, head_lanes(head * group_size + i)] = mixed[i * STEPS : (i + 1) * STEPS]


def stay_kernel(counts, hops_in, positions_in, kv, queries, fresh, cache, attended, own, *scratch):
    hops, positions, plan_sem, buffers, updated, blank, order, load_sems, store_sem = scratch
    load_plan((hops_in, positions_in), (hops, positions), plan_sem)
    slots = kv.shape[0]
    live = counts[0]
    stay = jnp.int32(0)
    for s in range(slots):
        staying = (s < live) & (hops[s] == 0)

        @pl.when(staying)
        def _(s=s, stay=stay):
            order[stay] = s
            pltpu.make_async_copy(kv.at[s], buffers.at[stay], load_sems.at[stay]).start()

        stay = stay + jnp.where(staying, 1, 0)

    own[...] = plan_row(hops, live, slots, own.shape)
    blank[...] = jnp.zeros_like(blank)

    def clear(j, carry):
        pltpu.make_async_copy(blank, cache.at[j], store_sem).start()
        attended[j] = jnp.zeros(attended.shape[1:], attended.dtype)
        return carry

    lax.fori_loop(stay, slots, clear, 0)

    def work(j, carry):
        pltpu.make_async_copy(kv.at[0], buffers.at[j], load_sems.at[j]).wait()

        def flush():
            pltpu.make_async_copy(updated.at[j], cache.at[j], store_sem).start()

        attend(
            buffers.at[j], updated.at[j], False, positions[order[j]], queries.at[j], fresh.at[j], attended.at[j], flush
        )
        return carry

    lax.fori_loop(0, stay, work, 0)

    def drain(j, carry):
        pltpu.make_async_copy(blank, cache.at[0], store_sem).wait()
        return carry

    lax.fori_loop(0, slots, drain, 0)


def arrive_kernel(mine, last, own, queries, fresh, cache_in, attended_in, *refs):
    del cache_in, attended_in
    seen = OFFSETS[: OFFSETS.index(mine[-1]) + 1]
    blocks, refs = dict(zip(seen, refs)), refs[len(seen) :]
    if last:
        known, cache, attended, served, buffers, heads, store_sems, total, total_sem = refs
    else:
        cache, attended, buffers, heads, store_sems = refs
    headers = {offset: header_of(block) for offset, block in blocks.items()}

    def entry(header, lane):
        shape = header[0:1].shape
        return jnp.sum(jnp.where(lane_iota(shape) == lane, header[0:1], 0))

    places = {}
    place = entry(own[...], STAY)
    for k, offset in enumerate(seen):
        present = entry(headers[offset], SENT + k) > 0
        places[offset] = (present, place)
        place = place + jnp.where(present, 1, 0)

    def stores(i, slot):
        return (
            pltpu.make_async_copy(buffers.at[i], cache.at[slot], store_sems.at[i, 0]),
            pltpu.make_async_copy(heads.at[i], attended.at[slot], store_sems.at[i, 1]),
        )

    for i, offset in enumerate(mine):
        present, slot = places[offset]

        @pl.when(present)
        def _(i=i, slot=slot, offset=offset):
            into_cache, into_attended = stores(i, slot)
            position = entry(headers[offset], POS)
            attend(
                blocks[offset],
                buffers.at[i],
                True,
                position,
                queries.at[slot],
                fresh.at[slot],
                heads.at[i],
                into_cache.start,
            )
            into_attended.start()

    if last:
        groups = known.shape[0]
        here = lax.axis_index("grp")
        rows = known[...]
        for offset in OFFSETS:
            rows = with_row(rows, lax.rem(here - offset + groups, groups), headers[offset])
        total[...] = count_served(rows)
        into_served = pltpu.make_async_copy(total, served, total_sem)
        into_served.start()

    for i, offset in enumerate(mine):
        present, slot = places[offset]

        @pl.when(present)
        def _(i=i, slot=slot):
            for copy in stores(i, slot):
                copy.wait()

    if last:
        into_served.wait()


def count_served(rows):
    groups = rows.shape[0]

    def column(lane, shift):
        moved = pltpu.roll(rows, shift % groups, 0) if shift % groups else rows
        return jnp.sum(jnp.where(lane_iota(rows.shape) == lane, moved, 0), axis=1, keepdims=True)

    total = column(STAY, 0)
    for k, offset in enumerate(OFFSETS):
        total = total + column(SENT + k, offset)
    square = (groups, groups)
    return jnp.sum(jnp.where(row_iota(square) == lane_iota(square), total, 0), axis=0)


def per_device(counts, hop_offsets, write_pos, kv_cache, queries, fresh_kv):
    groups = lax.axis_size("grp")
    slots = kv_cache.shape[0]
    stream = kv_cache.shape[1:]
    head_row = queries.shape[1:]
    params = pltpu.CompilerParams(vmem_limit_bytes=VMEM_LIMIT)
    plan = [counts, *(pltpu.with_memory_space_constraint(a, pltpu.HBM) for a in (hop_offsets, write_pos, kv_cache))]
    plan_scratch = [
        pltpu.SMEM(hop_offsets.shape, jnp.int32),
        pltpu.SMEM(write_pos.shape, jnp.int32),
        pltpu.SemaphoreType.DMA,
    ]
    block = jax.ShapeDtypeStruct(stream, kv_cache.dtype)
    table = jax.ShapeDtypeStruct((groups, LANES), jnp.int32)
    cache = jax.ShapeDtypeStruct(kv_cache.shape, kv_cache.dtype)
    heads = jax.ShapeDtypeStruct(queries.shape, queries.dtype)
    arrived = {}
    for offsets in PACKS:
        blocks = pl.pallas_call(
            functools.partial(pack_kernel, offsets),
            out_shape=[block] * len(offsets),
            in_specs=[SMEM_SPEC] + [HBM_SPEC] * 3,
            out_specs=[VMEM_SPEC] * len(offsets),
            scratch_shapes=plan_scratch + [pltpu.SemaphoreType.DMA((len(offsets),))],
            compiler_params=params,
            name="pack",
        )(*plan)
        for offset, outgoing in zip(offsets, blocks):
            arrived[offset] = shifted(outgoing, offset)

    new_cache, attended, own = pl.pallas_call(
        stay_kernel,
        out_shape=[cache, heads, jax.ShapeDtypeStruct((1, LANES), jnp.int32)],
        in_specs=[SMEM_SPEC] + [HBM_SPEC] * 3 + [VMEM_SPEC, VMEM_SPEC],
        out_specs=[ANY_SPEC, VMEM_SPEC, VMEM_SPEC],
        scratch_shapes=plan_scratch
        + [
            pltpu.VMEM(kv_cache.shape, kv_cache.dtype),
            pltpu.VMEM(kv_cache.shape, kv_cache.dtype),
            pltpu.VMEM(stream, kv_cache.dtype),
            pltpu.SMEM((slots,), jnp.int32),
            pltpu.SemaphoreType.DMA((slots,)),
            pltpu.SemaphoreType.DMA,
        ],
        compiler_params=params,
        cost_estimate=pl.CostEstimate(flops=50_000_000, bytes_accessed=4 * kv_cache.size, transcendentals=0),
        name="stay",
    )(*plan, queries, fresh_kv)

    known = pl.pallas_call(
        relay_kernel,
        out_shape=table,
        in_specs=[VMEM_SPEC] * (1 + len(NEAR)),
        out_specs=VMEM_SPEC,
        compiler_params=params,
        name="relay",
    )(own, *[arrived[offset] for offset in NEAR])
    for distance in relay_shifts(groups):
        known = jnp.maximum(known, shifted(known, distance))

    for mine in ARRIVALS:
        last = mine[-1] == OFFSETS[-1]
        new_cache, attended, *served = pl.pallas_call(
            functools.partial(arrive_kernel, mine, last),
            out_shape=[cache, heads] + [jax.ShapeDtypeStruct((groups,), jnp.int32)] * last,
            in_specs=[VMEM_SPEC] * 3 + [ANY_SPEC] * 2 + [VMEM_SPEC] * (OFFSETS.index(mine[-1]) + 1 + last),
            out_specs=[ANY_SPEC] * (2 + last),
            scratch_shapes=[
                pltpu.VMEM((len(mine),) + stream, kv_cache.dtype),
                pltpu.VMEM((len(mine),) + head_row, queries.dtype),
                pltpu.SemaphoreType.DMA((len(mine), 2)),
            ]
            + [pltpu.VMEM((groups,), jnp.int32), pltpu.SemaphoreType.DMA] * last,
            input_output_aliases={3: 0, 4: 1},
            compiler_params=params,
            name="arrive",
        )(
            own,
            queries,
            fresh_kv,
            new_cache,
            attended,
            *[arrived[offset] for offset in OFFSETS if offset <= mine[-1]],
            *[known] * last,
        )
    return (new_cache, attended, served[0])


def solution(mesh):
    return jax.shard_map(
        per_device,
        mesh=mesh,
        in_specs=(
            P(("rep", "grp")),
            P(("rep", "grp")),
            P(("rep", "grp")),
            P(("rep", "grp"), None, None, "tp"),
            P(("rep", "grp"), None, "tp"),
            P(("rep", "grp"), None, None, "tp"),
        ),
        out_specs=(P(("rep", "grp"), None, None, "tp"), P(("rep", "grp"), None, "tp"), P("rep")),
        check_vma=False,
    )
```

profile of v0, /device:TPU:0, one launch (start us, length us, event | category | flops | bytes accessed | tf_op | source)
XLA Modules:
  0.0 27.0 jit_solution(15703178217158480663)
XLA Ops:
  1.3 0.0 copy-start
  1.3 0.0 copy-start.1
  1.3 1.9 %pack.2 = (bf16[2,128,512]{2,1,0:T(8,128)(2,1)S(1)}, bf16[2,128,512]{2,1,0:T(8,128)(2,1)S(1)}) custom-call(s32[1]{0:T(128)S(6)} %copy.17.counts, s32[8]{0:T(128)} %hops_in.5, s32[8]{0:T(128)} %positions_in.5, bf16[8,2,128,512]{3,2,1,0:T(8,128)(2,1)} %kv.5), custom_call_target="tpu_custom_call" | custom-call | tf_op jit(solution)/shard_map/pack/pallas_call | solution.py:321
  3.2 5.1 %collective-permute-start = (bf16[2,128,512]{2,1,0:T(8,128)(2,1)S(1)}, bf16[2,128,512]{2,1,0:T(8,128)(2,1)S(1)}, u32[]{:S(2)}, u32[]{:S(2)}) collective-permute-start(bf16[2,128,512]{2,1,0:T(8,128)(2,1)S(1)} %get-tuple-element.15), channel_id=1, source_target_pairs={{0,12},{2,14},{4,0},{6,2},{8,4},{10,6},{12,8},{14,10},{1,13},{3,15... | collective-permute-start | bytes 786440 | tf_op jit(solution)/shard_map/ppermute | solution.py:33
  8.3 1.4 %collective-permute-start.1 = (bf16[2,128,512]{2,1,0:T(8,128)(2,1)S(1)}, bf16[2,128,512]{2,1,0:T(8,128)(2,1)S(1)}, u32[]{:S(2)}, u32[]{:S(2)}) collective-permute-start(bf16[2,128,512]{2,1,0:T(8,128)(2,1)S(1)} %get-tuple-element.16), channel_id=1, source_target_pairs={{0,14},{2,0},{4,2},{6,4},{8,6},{10,8},{12,10},{14,12},{1,15},{3,1}... | collective-permute-start | bytes 786440 | tf_op jit(solution)/shard_map/ppermute | solution.py:33
  9.7 1.8 %pack.3 = (bf16[2,128,512]{2,1,0:T(8,128)(2,1)S(1)}, bf16[2,128,512]{2,1,0:T(8,128)(2,1)S(1)}) custom-call(s32[1]{0:T(128)S(6)} %copy.17.counts, s32[8]{0:T(128)} %hops_in.5, s32[8]{0:T(128)} %positions_in.5, bf16[8,2,128,512]{3,2,1,0:T(8,128)(2,1)} %kv.5), custom_call_target="tpu_custom_call" | custom-call | tf_op jit(solution)/shard_map/pack/pallas_call | solution.py:321
  11.4 0.7 %collective-permute-start.2 = (bf16[2,128,512]{2,1,0:T(8,128)(2,1)S(1)}, bf16[2,128,512]{2,1,0:T(8,128)(2,1)S(1)}, u32[]{:S(2)}, u32[]{:S(2)}) collective-permute-start(bf16[2,128,512]{2,1,0:T(8,128)(2,1)S(1)} %get-tuple-element.17), channel_id=1, source_target_pairs={{0,2},{2,4},{4,6},{6,8},{8,10},{10,12},{12,14},{14,0},{1,3},{3,5},... | collective-permute-start | bytes 786440 | tf_op jit(solution)/shard_map/ppermute | solution.py:33
  12.1 1.0 %collective-permute-start.3 = (bf16[2,128,512]{2,1,0:T(8,128)(2,1)S(1)}, bf16[2,128,512]{2,1,0:T(8,128)(2,1)S(1)}, u32[]{:S(2)}, u32[]{:S(2)}) collective-permute-start(bf16[2,128,512]{2,1,0:T(8,128)(2,1)S(1)} %get-tuple-element.20), channel_id=1, source_target_pairs={{0,4},{2,6},{4,8},{6,10},{8,12},{10,14},{12,0},{14,2},{1,5},{3,7},... | collective-permute-start | bytes 786440 | tf_op jit(solution)/shard_map/ppermute | solution.py:33
  13.1 0.0 copy-done
  13.1 0.0 copy-done.1
  13.1 4.8 %stay.1 = (bf16[8,2,128,512]{3,2,1,0:T(8,128)(2,1)}, bf16[8,2,4096]{2,1,0:T(2,128)(2,1)}, s32[1,128]{1,0:T(1,128)S(1)}) custom-call(s32[1]{0:T(128)S(6)} %copy.17.counts, s32[8]{0:T(128)} %hops_in.5, s32[8]{0:T(128)} %positions_in.5, bf16[8,2,128,512]{3,2,1,0:T(8,128)(2,1)} %kv.5, bf16[8,2,4096]{2,1,0:T(2,128)(2,1)S(1)} %copy-done, ...), custom_call_target="tpu_custom_call" | custom-call | flops 50000000 | bytes 4194304 | tf_op jit(solution)/shard_map/stay/pallas_call | solution.py:333
  17.9 0.0 collective-permute-done.refs_0_.refs_1_
  17.9 2.8 %collective-permute-done.1.refs_1_.refs_0_ = bf16[2,128,512]{2,1,0:T(8,128)(2,1)S(1)} collective-permute-done((bf16[2,128,512]{2,1,0:T(8,128)(2,1)S(1)}, bf16[2,128,512]{2,1,0:T(8,128)(2,1)S(1)}, u32[]{:S(2)}, u32[]{:S(2)}) %collective-permute-start.1) | collective-permute-done | bytes 262176 | tf_op jit(solution)/shard_map/ppermute | solution.py:33
  20.7 2.4 %collective-permute-start.4 = (s32[8,128]{1,0:T(8,128)S(1)}, s32[8,128]{1,0:T(8,128)S(1)}, u32[]{:S(2)}, u32[]{:S(2)}) collective-permute-start(s32[8,128]{1,0:T(8,128)S(1)} %relay.1), channel_id=1, source_target_pairs={{0,10},{2,12},{4,14},{6,0},{8,2},{10,4},{12,6},{14,8},{1,11},{3,13... | collective-permute-start | bytes 12296 | tf_op jit(solution)/shard_map/ppermute | solution.py:33
  23.1 0.4 %collective-permute-done.2.refs_2_ = bf16[2,128,512]{2,1,0:T(8,128)(2,1)S(1)} collective-permute-done((bf16[2,128,512]{2,1,0:T(8,128)(2,1)S(1)}, bf16[2,128,512]{2,1,0:T(8,128)(2,1)S(1)}, u32[]{:S(2)}, u32[]{:S(2)}) %collective-permute-start.2) | collective-permute-done | bytes 262176 | tf_op jit(solution)/shard_map/ppermute | solution.py:33
  23.5 1.5 %arrive.2 = (bf16[8,2,128,512]{3,2,1,0:T(8,128)(2,1)}, bf16[8,2,4096]{2,1,0:T(2,128)(2,1)}) custom-call(s32[1,128]{1,0:T(1,128)S(1)} %get-tuple-element.12.own, bf16[8,2,4096]{2,1,0:T(2,128)(2,1)S(1)} %copy-done, bf16[8,2,2,512]{3,2,1,0:T(2,128)(2,1)S(1)} %copy-done.1, ...), custom_call_target="tpu_custom_call", output_to_operand_aliasing={{0}: (3, {}), {1}: (4, {})} | custom-call | tf_op jit(solution)/shard_map/arrive/pallas_call | solution.py:365
  25.0 0.6 %collective-permute-done.4 = s32[8,128]{1,0:T(8,128)S(1)} collective-permute-done((s32[8,128]{1,0:T(8,128)S(1)}, s32[8,128]{1,0:T(8,128)S(1)}, u32[]{:S(2)}, u32[]{:S(2)}) %collective-permute-start.4) | collective-permute-done | bytes 4128 | tf_op jit(solution)/shard_map/ppermute | solution.py:33
  25.6 0.5 %collective-permute-done.3.refs_3_ = bf16[2,128,512]{2,1,0:T(8,128)(2,1)S(1)} collective-permute-done((bf16[2,128,512]{2,1,0:T(8,128)(2,1)S(1)}, bf16[2,128,512]{2,1,0:T(8,128)(2,1)S(1)}, u32[]{:S(2)}, u32[]{:S(2)}) %collective-permute-start.3) | collective-permute-done | bytes 262176 | tf_op jit(solution)/shard_map/ppermute | solution.py:33
  26.2 0.8 %arrive.3 = (bf16[8,2,128,512]{3,2,1,0:T(8,128)(2,1)}, bf16[8,2,4096]{2,1,0:T(2,128)(2,1)}, s32[8]{0:T(128)}) custom-call(s32[1,128]{1,0:T(1,128)S(1)} %get-tuple-element.12.own, bf16[8,2,4096]{2,1,0:T(2,128)(2,1)S(1)} %copy-done, bf16[8,2,2,512]{3,2,1,0:T(2,128)(2,1)S(1)} %copy-done.1, ...), custom_call_target="tpu_custom_call", output_to_operand_aliasing={{0}: (3, {}), {1}: (4, {})} | custom-call | tf_op jit(solution)/shard_map/arrive/pallas_call | solution.py:365
  (2 shorter events, 0.0 us)
Async XLA Ops:
  1.3 11.9 %copy-start = (bf16[8,2,4096]{2,1,0:T(2,128)(2,1)S(1)}, bf16[8,2,4096]{2,1,0:T(2,128)(2,1)}, u32[]{:S(2)}) copy-start(bf16[8,2,4096]{2,1,0:T(2,128)(2,1)} %queries.5) | copy-start | bytes 393220
  1.3 11.8 %copy-start.1 = (bf16[8,2,2,512]{3,2,1,0:T(2,128)(2,1)S(1)}, bf16[8,2,2,512]{3,2,1,0:T(2,128)(2,1)}, u32[]{:S(2)}) copy-start(bf16[8,2,2,512]{3,2,1,0:T(2,128)(2,1)} %fresh.5) | copy-start | bytes 98308
  3.2 14.7 %collective-permute-start = (bf16[2,128,512]{2,1,0:T(8,128)(2,1)S(1)}, bf16[2,128,512]{2,1,0:T(8,128)(2,1)S(1)}, u32[]{:S(2)}, u32[]{:S(2)}) collective-permute-start(bf16[2,128,512]{2,1,0:T(8,128)(2,1)S(1)} %get-tuple-element.15), channel_id=1, source_target_pairs={{0,12},{2,14},{4,0},{6,2},{8,4},{10,6},{12,8},{14,10},{1,13},{3,15... | collective-permute-start | bytes 786440 | tf_op jit(solution)/shard_map/ppermute | solution.py:33
  8.3 12.4 %collective-permute-start.1 = (bf16[2,128,512]{2,1,0:T(8,128)(2,1)S(1)}, bf16[2,128,512]{2,1,0:T(8,128)(2,1)S(1)}, u32[]{:S(2)}, u32[]{:S(2)}) collective-permute-start(bf16[2,128,512]{2,1,0:T(8,128)(2,1)S(1)} %get-tuple-element.16), channel_id=1, source_target_pairs={{0,14},{2,0},{4,2},{6,4},{8,6},{10,8},{12,10},{14,12},{1,15},{3,1}... | collective-permute-start | bytes 786440 | tf_op jit(solution)/shard_map/ppermute | solution.py:33
  11.4 12.1 %collective-permute-start.2 = (bf16[2,128,512]{2,1,0:T(8,128)(2,1)S(1)}, bf16[2,128,512]{2,1,0:T(8,128)(2,1)S(1)}, u32[]{:S(2)}, u32[]{:S(2)}) collective-permute-start(bf16[2,128,512]{2,1,0:T(8,128)(2,1)S(1)} %get-tuple-element.17), channel_id=1, source_target_pairs={{0,2},{2,4},{4,6},{6,8},{8,10},{10,12},{12,14},{14,0},{1,3},{3,5},... | collective-permute-start | bytes 786440 | tf_op jit(solution)/shard_map/ppermute | solution.py:33
  12.1 14.0 %collective-permute-start.3 = (bf16[2,128,512]{2,1,0:T(8,128)(2,1)S(1)}, bf16[2,128,512]{2,1,0:T(8,128)(2,1)S(1)}, u32[]{:S(2)}, u32[]{:S(2)}) collective-permute-start(bf16[2,128,512]{2,1,0:T(8,128)(2,1)S(1)} %get-tuple-element.20), channel_id=1, source_target_pairs={{0,4},{2,6},{4,8},{6,10},{8,12},{10,14},{12,0},{14,2},{1,5},{3,7},... | collective-permute-start | bytes 786440 | tf_op jit(solution)/shard_map/ppermute | solution.py:33
  20.7 4.9 %collective-permute-start.4 = (s32[8,128]{1,0:T(8,128)S(1)}, s32[8,128]{1,0:T(8,128)S(1)}, u32[]{:S(2)}, u32[]{:S(2)}) collective-permute-start(s32[8,128]{1,0:T(8,128)S(1)} %relay.1), channel_id=1, source_target_pairs={{0,10},{2,12},{4,14},{6,0},{8,2},{10,4},{12,6},{14,8},{1,11},{3,13... | collective-permute-start | bytes 12296 | tf_op jit(solution)/shard_map/ppermute | solution.py:33
where the time goes:
time: 27.2 us; the launch traced here: 27 us
  Pallas kernels  10.7 us (39%)
  starting transfers between devices  10.5 us (39%)
  waiting for transfers between devices  4.39 us (16%)
  between operations  1.34 us (5%)
    ppermute x5, starting transfers between devices, shifted(): lax.ppermute(block, 'grp', [(i, (i + distance) % count) for i in range(co...  10.5 us
    pallas_call x1, Pallas kernels, per_device(): pl.pallas_call(stay_kernel, out_shape=[cache, heads, jax.ShapeDtypeStruct...  4.76 us
    ppermute x5, waiting for transfers between devices, shifted(): lax.ppermute(block, 'grp', [(i, (i + distance) % count) for i in range(co...  4.39 us
    pallas_call x2, Pallas kernels, per_device(): pl.pallas_call(functools.partial(pack_kernel, offsets), out_shape=[block]...  3.64 us
    pallas_call x2, Pallas kernels, per_device(): pl.pallas_call(functools.partial(arrive_kernel, mine, last), out_shape=[c...  2.27 us
  transfers between devices with their start and end apart: 5, of which 4 were waited for; matrix products, arithmetic and copies ran while one was open for 0% of the time, Pallas kernels for 30%

commit v1 on v0

--- a/solution.py
+++ b/solution.py
@@ -12,7 +12,7 @@
 REACH = 2
 STEPS = 2
 OFFSETS = tuple(o for o in range(-REACH, REACH + 1) if o != 0)
-PACKS = ((-2, -1), (1, 2))
+PACKS = ((-2, -1), (1,), (2,))
 NEAR = (-1, -2)
 ARRIVALS = ((-2, -1, 1), (2,))
 PATCH = 16
@@ -44,8 +44,8 @@
     return shifts
 
 
-def load_plan(sources, targets, sem):
-    copies = [pltpu.make_async_copy(a, b, sem) for a, b in zip(sources, targets)]
+def load_plan(sources, targets, sems):
+    copies = [pltpu.make_async_copy(a, b, sems.at[i]) for i, (a, b) in enumerate(zip(sources, targets))]
     for copy in copies:
         copy.start()
     for copy in copies:
@@ -84,8 +84,8 @@
 
 def pack_kernel(offsets, counts, hops_in, positions_in, kv, *refs):
     blocks = refs[: len(offsets)]
-    hops, positions, plan_sem, sems = refs[len(offsets) :]
-    load_plan((hops_in, positions_in), (hops, positions), plan_sem)
+    hops, positions, plan_sems, sems = refs[len(offsets) :]
+    load_plan((hops_in, positions_in), (hops, positions), plan_sems)
     slots, _, cache_len, _ = kv.shape
     picks, copies = [], []
     for k, offset in enumerate(offsets):
@@ -173,8 +173,8 @@
 
 
 def stay_kernel(counts, hops_in, positions_in, kv, queries, fresh, cache, attended, own, *scratch):
-    hops, positions, plan_sem, buffers, updated, blank, order, load_sems, store_sem = scratch
-    load_plan((hops_in, positions_in), (hops, positions), plan_sem)
+    hops, positions, plan_sems, buffers, updated, blank, order, load_sems, store_sems = scratch
+    load_plan((hops_in, positions_in), (hops, positions), plan_sems)
     slots = kv.shape[0]
     live = counts[0]
     stay = jnp.int32(0)
@@ -192,7 +192,7 @@
     blank[...] = jnp.zeros_like(blank)
 
     def clear(j, carry):
-        pltpu.make_async_copy(blank, cache.at[j], store_sem).start()
+        pltpu.make_async_copy(blank, cache.at[j], store_sems.at[j]).start()
         attended[j] = jnp.zeros(attended.shape[1:], attended.dtype)
         return carry
 
@@ -202,7 +202,7 @@
         pltpu.make_async_copy(kv.at[0], buffers.at[j], load_sems.at[j]).wait()
 
         def flush():
-            pltpu.make_async_copy(updated.at[j], cache.at[j], store_sem).start()
+            pltpu.make_async_copy(updated.at[j], cache.at[j], store_sems.at[j]).start()
 
         attend(
             buffers.at[j], updated.at[j], False, positions[order[j]], queries.at[j], fresh.at[j], attended.at[j], flush
@@ -212,7 +212,7 @@
     lax.fori_loop(0, stay, work, 0)
 
     def drain(j, carry):
-        pltpu.make_async_copy(blank, cache.at[0], store_sem).wait()
+        pltpu.make_async_copy(blank, cache.at[j], store_sems.at[j]).wait()
         return carry
 
     lax.fori_loop(0, slots, drain, 0)
@@ -310,7 +310,7 @@
     plan_scratch = [
         pltpu.SMEM(hop_offsets.shape, jnp.int32),
         pltpu.SMEM(write_pos.shape, jnp.int32),
-        pltpu.SemaphoreType.DMA,
+        pltpu.SemaphoreType.DMA((2,)),
     ]
     block = jax.ShapeDtypeStruct(stream, kv_cache.dtype)
     table = jax.ShapeDtypeStruct((groups, LANES), jnp.int32)
@@ -342,7 +342,7 @@
             pltpu.VMEM(stream, kv_cache.dtype),
             pltpu.SMEM((slots,), jnp.int32),
             pltpu.SemaphoreType.DMA((slots,)),
-            pltpu.SemaphoreType.DMA,
+            pltpu.SemaphoreType.DMA((slots,)),
         ],
         compiler_params=params,
         cost_estimate=pl.CostEstimate(flops=50_000_000, bytes_accessed=4 * kv_cache.size, transcendentals=0),

time: 27.2 us -> 27.1 us (level)
    pallas_call x1, Pallas kernels: 4.76 us -> 3.28 us  [per_device(): pl.pallas_call(stay_kernel, out_shape=[cache, heads, jax.ShapeDtypeStruct...]
    pallas_call x2 -> x3, Pallas kernels: 3.64 us -> 5.09 us  [per_device(): pl.pallas_call(functools.partial(pack_kernel, offsets), out_shape=[block]...]
where the time goes in v1:
time: 27.1 us; the launch traced here: 26.8 us
  Pallas kernels  10.7 us (39%)
  starting transfers between devices  10.6 us (39%)
  waiting for transfers between devices  4.27 us (16%)
  between operations  1.33 us (5%)
    ppermute x5, starting transfers between devices, shifted(): lax.ppermute(block, 'grp', [(i, (i + distance) % count) for i in range(co...  10.6 us
    pallas_call x3, Pallas kernels, per_device(): pl.pallas_call(functools.partial(pack_kernel, offsets), out_shape=[block]...  5.09 us
    ppermute x5, waiting for transfers between devices, shifted(): lax.ppermute(block, 'grp', [(i, (i + distance) % count) for i in range(co...  4.27 us
    pallas_call x1, Pallas kernels, per_device(): pl.pallas_call(stay_kernel, out_shape=[cache, heads, jax.ShapeDtypeStruct...  3.28 us
    pallas_call x2, Pallas kernels, per_device(): pl.pallas_call(functools.partial(arrive_kernel, mine, last), out_shape=[c...  2.27 us
  transfers between devices with their start and end apart: 5, of which 4 were waited for; matrix products, arithmetic and copies ran while one was open for 0% of the time, Pallas kernels for 30%

profile of v1, /device:TPU:0, one launch (start us, length us, event | category | flops | bytes accessed | tf_op | source)
XLA Modules:
  0.0 26.8 jit_solution(10850404462518962333)
XLA Ops:
  1.3 1.8 %pack.3 = (bf16[2,128,512]{2,1,0:T(8,128)(2,1)S(1)}, bf16[2,128,512]{2,1,0:T(8,128)(2,1)S(1)}) custom-call(s32[1]{0:T(128)S(6)} %copy.17.counts, s32[8]{0:T(128)} %hops_in.7, s32[8]{0:T(128)} %positions_in.7, bf16[8,2,128,512]{3,2,1,0:T(8,128)(2,1)} %kv.7), custom_call_target="tpu_custom_call" | custom-call | tf_op jit(solution)/shard_map/pack/pallas_call | solution.py:321
  3.0 5.1 %collective-permute-start = (bf16[2,128,512]{2,1,0:T(8,128)(2,1)S(1)}, bf16[2,128,512]{2,1,0:T(8,128)(2,1)S(1)}, u32[]{:S(2)}, u32[]{:S(2)}) collective-permute-start(bf16[2,128,512]{2,1,0:T(8,128)(2,1)S(1)} %get-tuple-element.13), channel_id=1, source_target_pairs={{0,12},{2,14},{4,0},{6,2},{8,4},{10,6},{12,8},{14,10},{1,13},{3,15... | collective-permute-start | bytes 786440 | tf_op jit(solution)/shard_map/ppermute | solution.py:33
  8.2 0.0 copy-start
  8.2 0.0 copy-start.1
  8.2 1.4 %collective-permute-start.1 = (bf16[2,128,512]{2,1,0:T(8,128)(2,1)S(1)}, bf16[2,128,512]{2,1,0:T(8,128)(2,1)S(1)}, u32[]{:S(2)}, u32[]{:S(2)}) collective-permute-start(bf16[2,128,512]{2,1,0:T(8,128)(2,1)S(1)} %get-tuple-element.14), channel_id=1, source_target_pairs={{0,14},{2,0},{4,2},{6,4},{8,6},{10,8},{12,10},{14,12},{1,15},{3,1}... | collective-permute-start | bytes 786440 | tf_op jit(solution)/shard_map/ppermute | solution.py:33
  9.5 1.7 %pack.4 = bf16[2,128,512]{2,1,0:T(8,128)(2,1)S(1)} custom-call(s32[1]{0:T(128)S(6)} %copy.17.counts, s32[8]{0:T(128)} %hops_in.7, s32[8]{0:T(128)} %positions_in.7, bf16[8,2,128,512]{3,2,1,0:T(8,128)(2,1)} %kv.7), custom_call_target="tpu_custom_call" | custom-call | tf_op jit(solution)/shard_map/pack/pallas_call | solution.py:321
  11.2 0.7 %collective-permute-start.2 = (bf16[2,128,512]{2,1,0:T(8,128)(2,1)S(1)}, bf16[2,128,512]{2,1,0:T(8,128)(2,1)S(1)}, u32[]{:S(2)}, u32[]{:S(2)}) collective-permute-start(bf16[2,128,512]{2,1,0:T(8,128)(2,1)S(1)} %pack.4), channel_id=1, source_target_pairs={{0,2},{2,4},{4,6},{6,8},{8,10},{10,12},{12,14},{14,0},{1,3},{3,5},... | collective-permute-start | bytes 786440 | tf_op jit(solution)/shard_map/ppermute | solution.py:33
  11.9 1.7 %pack.5 = bf16[2,128,512]{2,1,0:T(8,128)(2,1)S(1)} custom-call(s32[1]{0:T(128)S(6)} %copy.17.counts, s32[8]{0:T(128)} %hops_in.7, s32[8]{0:T(128)} %positions_in.7, bf16[8,2,128,512]{3,2,1,0:T(8,128)(2,1)} %kv.7), custom_call_target="tpu_custom_call" | custom-call | tf_op jit(solution)/shard_map/pack/pallas_call | solution.py:321
  13.6 1.0 %collective-permute-start.3 = (bf16[2,128,512]{2,1,0:T(8,128)(2,1)S(1)}, bf16[2,128,512]{2,1,0:T(8,128)(2,1)S(1)}, u32[]{:S(2)}, u32[]{:S(2)}) collective-permute-start(bf16[2,128,512]{2,1,0:T(8,128)(2,1)S(1)} %pack.5), channel_id=1, source_target_pairs={{0,4},{2,6},{4,8},{6,10},{8,12},{10,14},{12,0},{14,2},{1,5},{3,7},... | collective-permute-start | bytes 786440 | tf_op jit(solution)/shard_map/ppermute | solution.py:33
  14.6 0.0 copy-done
  14.6 0.0 copy-done.1
  14.6 3.3 %stay.1 = (bf16[8,2,128,512]{3,2,1,0:T(8,128)(2,1)}, bf16[8,2,4096]{2,1,0:T(2,128)(2,1)}, s32[1,128]{1,0:T(1,128)S(1)}) custom-call(s32[1]{0:T(128)S(6)} %copy.17.counts, s32[8]{0:T(128)} %hops_in.7, s32[8]{0:T(128)} %positions_in.7, bf16[8,2,128,512]{3,2,1,0:T(8,128)(2,1)} %kv.7, bf16[8,2,4096]{2,1,0:T(2,128)(2,1)S(1)} %copy-done, ...), custom_call_target="tpu_custom_call" | custom-call | flops 50000000 | bytes 4194304 | tf_op jit(solution)/shard_map/stay/pallas_call | solution.py:333
  17.9 0.0 collective-permute-done.refs_0_.refs_1_
  17.9 2.7 %collective-permute-done.1.refs_1_.refs_0_ = bf16[2,128,512]{2,1,0:T(8,128)(2,1)S(1)} collective-permute-done((bf16[2,128,512]{2,1,0:T(8,128)(2,1)S(1)}, bf16[2,128,512]{2,1,0:T(8,128)(2,1)S(1)}, u32[]{:S(2)}, u32[]{:S(2)}) %collective-permute-start.1) | collective-permute-done | bytes 262176 | tf_op jit(solution)/shard_map/ppermute | solution.py:33
  20.6 2.4 %collective-permute-start.4 = (s32[8,128]{1,0:T(8,128)S(1)}, s32[8,128]{1,0:T(8,128)S(1)}, u32[]{:S(2)}, u32[]{:S(2)}) collective-permute-start(s32[8,128]{1,0:T(8,128)S(1)} %relay.1), channel_id=1, source_target_pairs={{0,10},{2,12},{4,14},{6,0},{8,2},{10,4},{12,6},{14,8},{1,11},{3,13... | collective-permute-start | bytes 12296 | tf_op jit(solution)/shard_map/ppermute | solution.py:33
  23.0 0.3 %collective-permute-done.2.refs_2_ = bf16[2,128,512]{2,1,0:T(8,128)(2,1)S(1)} collective-permute-done((bf16[2,128,512]{2,1,0:T(8,128)(2,1)S(1)}, bf16[2,128,512]{2,1,0:T(8,128)(2,1)S(1)}, u32[]{:S(2)}, u32[]{:S(2)}) %collective-permute-start.2) | collective-permute-done | bytes 262176 | tf_op jit(solution)/shard_map/ppermute | solution.py:33
  23.3 1.5 %arrive.2 = (bf16[8,2,128,512]{3,2,1,0:T(8,128)(2,1)}, bf16[8,2,4096]{2,1,0:T(2,128)(2,1)}) custom-call(s32[1,128]{1,0:T(1,128)S(1)} %get-tuple-element.10.own, bf16[8,2,4096]{2,1,0:T(2,128)(2,1)S(1)} %copy-done, bf16[8,2,2,512]{3,2,1,0:T(2,128)(2,1)S(1)} %copy-done.1, ...), custom_call_target="tpu_custom_call", output_to_operand_aliasing={{0}: (3, {}), {1}: (4, {})} | custom-call | tf_op jit(solution)/shard_map/arrive/pallas_call | solution.py:365
  24.8 0.7 %collective-permute-done.4 = s32[8,128]{1,0:T(8,128)S(1)} collective-permute-done((s32[8,128]{1,0:T(8,128)S(1)}, s32[8,128]{1,0:T(8,128)S(1)}, u32[]{:S(2)}, u32[]{:S(2)}) %collective-permute-start.4) | collective-permute-done | bytes 4128 | tf_op jit(solution)/shard_map/ppermute | solution.py:33
  25.5 0.5 %collective-permute-done.3.refs_3_ = bf16[2,128,512]{2,1,0:T(8,128)(2,1)S(1)} collective-permute-done((bf16[2,128,512]{2,1,0:T(8,128)(2,1)S(1)}, bf16[2,128,512]{2,1,0:T(8,128)(2,1)S(1)}, u32[]{:S(2)}, u32[]{:S(2)}) %collective-permute-start.3) | collective-permute-done | bytes 262176 | tf_op jit(solution)/shard_map/ppermute | solution.py:33
  26.0 0.8 %arrive.3 = (bf16[8,2,128,512]{3,2,1,0:T(8,128)(2,1)}, bf16[8,2,4096]{2,1,0:T(2,128)(2,1)}, s32[8]{0:T(128)}) custom-call(s32[1,128]{1,0:T(1,128)S(1)} %get-tuple-element.10.own, bf16[8,2,4096]{2,1,0:T(2,128)(2,1)S(1)} %copy-done, bf16[8,2,2,512]{3,2,1,0:T(2,128)(2,1)S(1)} %copy-done.1, ...), custom_call_target="tpu_custom_call", output_to_operand_aliasing={{0}: (3, {}), {1}: (4, {})} | custom-call | tf_op jit(solution)/shard_map/arrive/pallas_call | solution.py:365
  (2 shorter events, 0.0 us)
Async XLA Ops:
  3.0 14.8 %collective-permute-start = (bf16[2,128,512]{2,1,0:T(8,128)(2,1)S(1)}, bf16[2,128,512]{2,1,0:T(8,128)(2,1)S(1)}, u32[]{:S(2)}, u32[]{:S(2)}) collective-permute-start(bf16[2,128,512]{2,1,0:T(8,128)(2,1)S(1)} %get-tuple-element.13), channel_id=1, source_target_pairs={{0,12},{2,14},{4,0},{6,2},{8,4},{10,6},{12,8},{14,10},{1,13},{3,15... | collective-permute-start | bytes 786440 | tf_op jit(solution)/shard_map/ppermute | solution.py:33
  8.2 6.4 %copy-start = (bf16[8,2,4096]{2,1,0:T(2,128)(2,1)S(1)}, bf16[8,2,4096]{2,1,0:T(2,128)(2,1)}, u32[]{:S(2)}) copy-start(bf16[8,2,4096]{2,1,0:T(2,128)(2,1)} %queries.5) | copy-start | bytes 393220
  8.2 6.4 %copy-start.1 = (bf16[8,2,2,512]{3,2,1,0:T(2,128)(2,1)S(1)}, bf16[8,2,2,512]{3,2,1,0:T(2,128)(2,1)}, u32[]{:S(2)}) copy-start(bf16[8,2,2,512]{3,2,1,0:T(2,128)(2,1)} %fresh.5) | copy-start | bytes 98308
  8.2 12.4 %collective-permute-start.1 = (bf16[2,128,512]{2,1,0:T(8,128)(2,1)S(1)}, bf16[2,128,512]{2,1,0:T(8,128)(2,1)S(1)}, u32[]{:S(2)}, u32[]{:S(2)}) collective-permute-start(bf16[2,128,512]{2,1,0:T(8,128)(2,1)S(1)} %get-tuple-element.14), channel_id=1, source_target_pairs={{0,14},{2,0},{4,2},{6,4},{8,6},{10,8},{12,10},{14,12},{1,15},{3,1}... | collective-permute-start | bytes 786440 | tf_op jit(solution)/shard_map/ppermute | solution.py:33
  11.2 12.1 %collective-permute-start.2 = (bf16[2,128,512]{2,1,0:T(8,128)(2,1)S(1)}, bf16[2,128,512]{2,1,0:T(8,128)(2,1)S(1)}, u32[]{:S(2)}, u32[]{:S(2)}) collective-permute-start(bf16[2,128,512]{2,1,0:T(8,128)(2,1)S(1)} %pack.4), channel_id=1, source_target_pairs={{0,2},{2,4},{4,6},{6,8},{8,10},{10,12},{12,14},{14,0},{1,3},{3,5},... | collective-permute-start | bytes 786440 | tf_op jit(solution)/shard_map/ppermute | solution.py:33
  13.6 12.5 %collective-permute-start.3 = (bf16[2,128,512]{2,1,0:T(8,128)(2,1)S(1)}, bf16[2,128,512]{2,1,0:T(8,128)(2,1)S(1)}, u32[]{:S(2)}, u32[]{:S(2)}) collective-permute-start(bf16[2,128,512]{2,1,0:T(8,128)(2,1)S(1)} %pack.5), channel_id=1, source_target_pairs={{0,4},{2,6},{4,8},{6,10},{8,12},{10,14},{12,0},{14,2},{1,5},{3,7},... | collective-permute-start | bytes 786440 | tf_op jit(solution)/shard_map/ppermute | solution.py:33
  20.6 4.9 %collective-permute-start.4 = (s32[8,128]{1,0:T(8,128)S(1)}, s32[8,128]{1,0:T(8,128)S(1)}, u32[]{:S(2)}, u32[]{:S(2)}) collective-permute-start(s32[8,128]{1,0:T(8,128)S(1)} %relay.1), channel_id=1, source_target_pairs={{0,10},{2,12},{4,14},{6,0},{8,2},{10,4},{12,6},{14,8},{1,11},{3,13... | collective-permute-start | bytes 12296 | tf_op jit(solution)/shard_map/ppermute | solution.py:33

commit v2 on v1

--- a/solution.py
+++ b/solution.py
@@ -135,8 +135,14 @@
     group_size = queries.shape[-1] // width
     first = first_written(position, cache_len)
     second = first_written(position + 1, cache_len)
+    padding = jnp.zeros((PATCH - STEPS, HEAD_DIM), jnp.bfloat16)
+    scores = []
+    for head in range(head_count):
+        query = jnp.concatenate([queries[:, head_lanes(head * group_size + i)] for i in range(group_size)], axis=0)
+        keys = jnp.concatenate([old[0, :, head_lanes(head)], fresh[0][:, head_lanes(head)], padding], axis=0)
+        scores.append(lax.dot_general(query, keys, (((1,), (1,)), ((), ())), preferred_element_type=jnp.float32))
     for side in range(2):
-        written = fresh[side].astype(jnp.float32)
+        rows_now = fresh[side].astype(jnp.float32)
         for head in range(head_count):
             lanes = head_lanes(head)
             rows = old[side, :, lanes].astype(jnp.float32)
@@ -144,23 +150,24 @@
             if has_header and (side, head) == (0, 0):
                 top = jnp.sum(jnp.where(row == first, rows, 0.0), axis=0, keepdims=True)
                 rows = jnp.where(row == 0, top, rows)
-            rows = jnp.where(row == second, written[1:2, lanes], jnp.where(row == first, written[0:1, lanes], rows))
+            rows = jnp.where(row == second, rows_now[1:2, lanes], jnp.where(row == first, rows_now[0:1, lanes], rows))
             new[side, :, lanes] = rows.astype(jnp.bfloat16)
     flush()
 
     def both(side, head):
         return jnp.concatenate([new[side, :, head_lanes(head)], old[side, :, head_lanes(head)]], axis=0)
 
-    scores = []
-    for head in range(head_count):
-        query = jnp.concatenate([queries[:, head_lanes(head * group_size + i)] for i in range(group_size)], axis=0)
-        scores.append(
-            lax.dot_general(query, both(0, head), (((1,), (1,)), ((), ())), preferred_element_type=jnp.float32)
-        )
     scores = jnp.concatenate(scores, axis=0)
     shape = (scores.shape[0], cache_len)
-    stale = (row_iota(shape) % STEPS == 0) & (lane_iota(shape) == second)
-    scores = jnp.where(stale, scores[:, cache_len:], scores[:, :cache_len]) * HEAD_DIM ** (-0.5)
+    row, lane = row_iota(shape), lane_iota(shape)
+    stale = (row % STEPS == 0) & (lane == second)
+    written = [scores[:, cache_len + t : cache_len + t + 1] for t in range(STEPS)]
+    scores = scores[:, :cache_len]
+    if has_header:
+        top = jnp.sum(jnp.where(lane == first, scores, 0.0), axis=1, keepdims=True)
+        scores = jnp.where((lane == 0) & (row < group_size * STEPS), top, scores)
+    scores = jnp.where(lane == first, written[0], scores)
+    scores = jnp.where((lane == second) & jnp.logical_not(stale), written[1], scores) * HEAD_DIM ** (-0.5)
     weights = jnp.exp(scores - jnp.max(scores, axis=1, keepdims=True))
     weights = weights / jnp.sum(weights, axis=1, keepdims=True)
     weights = jnp.concatenate([jnp.where(stale, 0.0, weights), jnp.where(stale, weights, 0.0)], axis=1)
@@ -227,6 +234,16 @@
     else:
         cache, attended, buffers, heads, store_sems = refs
     headers = {offset: header_of(block) for offset, block in blocks.items()}
+
+    if last:
+        groups = known.shape[0]
+        here = lax.axis_index("grp")
+        rows = known[...]
+        for offset in OFFSETS:
+            rows = with_row(rows, lax.rem(here - offset + groups, groups), headers[offset])
+        total[...] = count_served(rows)
+        into_served = pltpu.make_async_copy(total, served, total_sem)
+        into_served.start()
 
     def entry(header, lane):
         shape = header[0:1].shape
@@ -263,16 +280,6 @@
                 into_cache.start,
             )
             into_attended.start()
-
-    if last:
-        groups = known.shape[0]
-        here = lax.axis_index("grp")
-        rows = known[...]
-        for offset in OFFSETS:
-            rows = with_row(rows, lax.rem(here - offset + groups, groups), headers[offset])
-        total[...] = count_served(rows)
-        into_served = pltpu.make_async_copy(total, served, total_sem)
-        into_served.start()
 
     for i, offset in enumerate(mine):
         present, slot = places[offset]

time: 27.1 us -> 27 us (level)
  transfers between devices with their start and end apart: 5 -> 5, of which waited for: 4 -> 4; matrix products, arithmetic and copies ran while one was open for 0% -> 0% of each run, Pallas kernels for 30% -> 31%
where the time goes in v2:
time: 27 us; the launch traced here: 26.7 us
  Pallas kernels  10.6 us (39%)
  starting transfers between devices  10.6 us (39%)
  waiting for transfers between devices  4.18 us (15%)
  between operations  1.33 us (5%)
    ppermute x5, starting transfers between devices, shifted(): lax.ppermute(block, 'grp', [(i, (i + distance) % count) for i in range(co...  10.6 us
    pallas_call x3, Pallas kernels, per_device(): pl.pallas_call(functools.partial(pack_kernel, offsets), out_shape=[block]...  5.09 us
    ppermute x5, waiting for transfers between devices, shifted(): lax.ppermute(block, 'grp', [(i, (i + distance) % count) for i in range(co...  4.18 us
    pallas_call x1, Pallas kernels, per_device(): pl.pallas_call(stay_kernel, out_shape=[cache, heads, jax.ShapeDtypeStruct...  3.4 us
    pallas_call x2, Pallas kernels, per_device(): pl.pallas_call(functools.partial(arrive_kernel, mine, last), out_shape=[c...  2.1 us
  transfers between devices with their start and end apart: 5, of which 4 were waited for; matrix products, arithmetic and copies ran while one was open for 0% of the time, Pallas kernels for 31%

profile of v2, /device:TPU:0, one launch (start us, length us, event | category | flops | bytes accessed | tf_op | source)
XLA Modules:
  0.0 26.7 jit_solution(2481359409854366420)
XLA Ops:
  1.3 1.8 %pack.3 = (bf16[2,128,512]{2,1,0:T(8,128)(2,1)S(1)}, bf16[2,128,512]{2,1,0:T(8,128)(2,1)S(1)}) custom-call(s32[1]{0:T(128)S(6)} %copy.17.counts, s32[8]{0:T(128)} %hops_in.7, s32[8]{0:T(128)} %positions_in.7, bf16[8,2,128,512]{3,2,1,0:T(8,128)(2,1)} %kv.7), custom_call_target="tpu_custom_call" | custom-call | tf_op jit(solution)/shard_map/pack/pallas_call | solution.py:328
  3.0 5.1 %collective-permute-start = (bf16[2,128,512]{2,1,0:T(8,128)(2,1)S(1)}, bf16[2,128,512]{2,1,0:T(8,128)(2,1)S(1)}, u32[]{:S(2)}, u32[]{:S(2)}) collective-permute-start(bf16[2,128,512]{2,1,0:T(8,128)(2,1)S(1)} %get-tuple-element.13), channel_id=1, source_target_pairs={{0,12},{2,14},{4,0},{6,2},{8,4},{10,6},{12,8},{14,10},{1,13},{3,15... | collective-permute-start | bytes 786440 | tf_op jit(solution)/shard_map/ppermute | solution.py:33
  8.2 0.0 copy-start
  8.2 0.0 copy-start.1
  8.2 1.4 %collective-permute-start.1 = (bf16[2,128,512]{2,1,0:T(8,128)(2,1)S(1)}, bf16[2,128,512]{2,1,0:T(8,128)(2,1)S(1)}, u32[]{:S(2)}, u32[]{:S(2)}) collective-permute-start(bf16[2,128,512]{2,1,0:T(8,128)(2,1)S(1)} %get-tuple-element.14), channel_id=1, source_target_pairs={{0,14},{2,0},{4,2},{6,4},{8,6},{10,8},{12,10},{14,12},{1,15},{3,1}... | collective-permute-start | bytes 786440 | tf_op jit(solution)/shard_map/ppermute | solution.py:33
  9.5 1.7 %pack.4 = bf16[2,128,512]{2,1,0:T(8,128)(2,1)S(1)} custom-call(s32[1]{0:T(128)S(6)} %copy.17.counts, s32[8]{0:T(128)} %hops_in.7, s32[8]{0:T(128)} %positions_in.7, bf16[8,2,128,512]{3,2,1,0:T(8,128)(2,1)} %kv.7), custom_call_target="tpu_custom_call" | custom-call | tf_op jit(solution)/shard_map/pack/pallas_call | solution.py:328
  11.2 0.7 %collective-permute-start.2 = (bf16[2,128,512]{2,1,0:T(8,128)(2,1)S(1)}, bf16[2,128,512]{2,1,0:T(8,128)(2,1)S(1)}, u32[]{:S(2)}, u32[]{:S(2)}) collective-permute-start(bf16[2,128,512]{2,1,0:T(8,128)(2,1)S(1)} %pack.4), channel_id=1, source_target_pairs={{0,2},{2,4},{4,6},{6,8},{8,10},{10,12},{12,14},{14,0},{1,3},{3,5},... | collective-permute-start | bytes 786440 | tf_op jit(solution)/shard_map/ppermute | solution.py:33
  11.9 1.7 %pack.5 = bf16[2,128,512]{2,1,0:T(8,128)(2,1)S(1)} custom-call(s32[1]{0:T(128)S(6)} %copy.17.counts, s32[8]{0:T(128)} %hops_in.7, s32[8]{0:T(128)} %positions_in.7, bf16[8,2,128,512]{3,2,1,0:T(8,128)(2,1)} %kv.7), custom_call_target="tpu_custom_call" | custom-call | tf_op jit(solution)/shard_map/pack/pallas_call | solution.py:328
  13.6 1.0 %collective-permute-start.3 = (bf16[2,128,512]{2,1,0:T(8,128)(2,1)S(1)}, bf16[2,128,512]{2,1,0:T(8,128)(2,1)S(1)}, u32[]{:S(2)}, u32[]{:S(2)}) collective-permute-start(bf16[2,128,512]{2,1,0:T(8,128)(2,1)S(1)} %pack.5), channel_id=1, source_target_pairs={{0,4},{2,6},{4,8},{6,10},{8,12},{10,14},{12,0},{14,2},{1,5},{3,7},... | collective-permute-start | bytes 786440 | tf_op jit(solution)/shard_map/ppermute | solution.py:33
  14.6 0.0 copy-done
  14.6 0.0 copy-done.1
  14.6 3.4 %stay.1 = (bf16[8,2,128,512]{3,2,1,0:T(8,128)(2,1)}, bf16[8,2,4096]{2,1,0:T(2,128)(2,1)}, s32[1,128]{1,0:T(1,128)S(1)}) custom-call(s32[1]{0:T(128)S(6)} %copy.17.counts, s32[8]{0:T(128)} %hops_in.7, s32[8]{0:T(128)} %positions_in.7, bf16[8,2,128,512]{3,2,1,0:T(8,128)(2,1)} %kv.7, bf16[8,2,4096]{2,1,0:T(2,128)(2,1)S(1)} %copy-done, ...), custom_call_target="tpu_custom_call" | custom-call | flops 50000000 | bytes 4194304 | tf_op jit(solution)/shard_map/stay/pallas_call | solution.py:340
  18.0 0.0 collective-permute-done.refs_0_.refs_1_
  18.0 2.6 %collective-permute-done.1.refs_1_.refs_0_ = bf16[2,128,512]{2,1,0:T(8,128)(2,1)S(1)} collective-permute-done((bf16[2,128,512]{2,1,0:T(8,128)(2,1)S(1)}, bf16[2,128,512]{2,1,0:T(8,128)(2,1)S(1)}, u32[]{:S(2)}, u32[]{:S(2)}) %collective-permute-start.1) | collective-permute-done | bytes 262176 | tf_op jit(solution)/shard_map/ppermute | solution.py:33
  20.6 2.4 %collective-permute-start.4 = (s32[8,128]{1,0:T(8,128)S(1)}, s32[8,128]{1,0:T(8,128)S(1)}, u32[]{:S(2)}, u32[]{:S(2)}) collective-permute-start(s32[8,128]{1,0:T(8,128)S(1)} %relay.1), channel_id=1, source_target_pairs={{0,10},{2,12},{4,14},{6,0},{8,2},{10,4},{12,6},{14,8},{1,11},{3,13... | collective-permute-start | bytes 12296 | tf_op jit(solution)/shard_map/ppermute | solution.py:33
  23.0 0.3 %collective-permute-done.2.refs_2_ = bf16[2,128,512]{2,1,0:T(8,128)(2,1)S(1)} collective-permute-done((bf16[2,128,512]{2,1,0:T(8,128)(2,1)S(1)}, bf16[2,128,512]{2,1,0:T(8,128)(2,1)S(1)}, u32[]{:S(2)}, u32[]{:S(2)}) %collective-permute-start.2) | collective-permute-done | bytes 262176 | tf_op jit(solution)/shard_map/ppermute | solution.py:33
  23.3 1.5 %arrive.2 = (bf16[8,2,128,512]{3,2,1,0:T(8,128)(2,1)}, bf16[8,2,4096]{2,1,0:T(2,128)(2,1)}) custom-call(s32[1,128]{1,0:T(1,128)S(1)} %get-tuple-element.10.own, bf16[8,2,4096]{2,1,0:T(2,128)(2,1)S(1)} %copy-done, bf16[8,2,2,512]{3,2,1,0:T(2,128)(2,1)S(1)} %copy-done.1, ...), custom_call_target="tpu_custom_call", output_to_operand_aliasing={{0}: (3, {}), {1}: (4, {})} | custom-call | tf_op jit(solution)/shard_map/arrive/pallas_call | solution.py:372
  24.7 0.7 %collective-permute-done.4 = s32[8,128]{1,0:T(8,128)S(1)} collective-permute-done((s32[8,128]{1,0:T(8,128)S(1)}, s32[8,128]{1,0:T(8,128)S(1)}, u32[]{:S(2)}, u32[]{:S(2)}) %collective-permute-start.4) | collective-permute-done | bytes 4128 | tf_op jit(solution)/shard_map/ppermute | solution.py:33
  25.5 0.5 %collective-permute-done.3.refs_3_ = bf16[2,128,512]{2,1,0:T(8,128)(2,1)S(1)} collective-permute-done((bf16[2,128,512]{2,1,0:T(8,128)(2,1)S(1)}, bf16[2,128,512]{2,1,0:T(8,128)(2,1)S(1)}, u32[]{:S(2)}, u32[]{:S(2)}) %collective-permute-start.3) | collective-permute-done | bytes 262176 | tf_op jit(solution)/shard_map/ppermute | solution.py:33
  26.0 0.7 %arrive.3 = (bf16[8,2,128,512]{3,2,1,0:T(8,128)(2,1)}, bf16[8,2,4096]{2,1,0:T(2,128)(2,1)}, s32[8]{0:T(128)}) custom-call(s32[1,128]{1,0:T(1,128)S(1)} %get-tuple-element.10.own, bf16[8,2,4096]{2,1,0:T(2,128)(2,1)S(1)} %copy-done, bf16[8,2,2,512]{3,2,1,0:T(2,128)(2,1)S(1)} %copy-done.1, ...), custom_call_target="tpu_custom_call", output_to_operand_aliasing={{0}: (3, {}), {1}: (4, {})} | custom-call | tf_op jit(solution)/shard_map/arrive/pallas_call | solution.py:372
  (2 shorter events, 0.0 us)
Async XLA Ops:
  3.0 14.9 %collective-permute-start = (bf16[2,128,512]{2,1,0:T(8,128)(2,1)S(1)}, bf16[2,128,512]{2,1,0:T(8,128)(2,1)S(1)}, u32[]{:S(2)}, u32[]{:S(2)}) collective-permute-start(bf16[2,128,512]{2,1,0:T(8,128)(2,1)S(1)} %get-tuple-element.13), channel_id=1, source_target_pairs={{0,12},{2,14},{4,0},{6,2},{8,4},{10,6},{12,8},{14,10},{1,13},{3,15... | collective-permute-start | bytes 786440 | tf_op jit(solution)/shard_map/ppermute | solution.py:33
  8.2 6.4 %copy-start = (bf16[8,2,4096]{2,1,0:T(2,128)(2,1)S(1)}, bf16[8,2,4096]{2,1,0:T(2,128)(2,1)}, u32[]{:S(2)}) copy-start(bf16[8,2,4096]{2,1,0:T(2,128)(2,1)} %queries.5) | copy-start | bytes 393220
  8.2 6.4 %copy-start.1 = (bf16[8,2,2,512]{3,2,1,0:T(2,128)(2,1)S(1)}, bf16[8,2,2,512]{3,2,1,0:T(2,128)(2,1)}, u32[]{:S(2)}) copy-start(bf16[8,2,2,512]{3,2,1,0:T(2,128)(2,1)} %fresh.5) | copy-start | bytes 98308
  8.2 12.4 %collective-permute-start.1 = (bf16[2,128,512]{2,1,0:T(8,128)(2,1)S(1)}, bf16[2,128,512]{2,1,0:T(8,128)(2,1)S(1)}, u32[]{:S(2)}, u32[]{:S(2)}) collective-permute-start(bf16[2,128,512]{2,1,0:T(8,128)(2,1)S(1)} %get-tuple-element.14), channel_id=1, source_target_pairs={{0,14},{2,0},{4,2},{6,4},{8,6},{10,8},{12,10},{14,12},{1,15},{3,1}... | collective-permute-start | bytes 786440 | tf_op jit(solution)/shard_map/ppermute | solution.py:33
  11.2 12.1 %collective-permute-start.2 = (bf16[2,128,512]{2,1,0:T(8,128)(2,1)S(1)}, bf16[2,128,512]{2,1,0:T(8,128)(2,1)S(1)}, u32[]{:S(2)}, u32[]{:S(2)}) collective-permute-start(bf16[2,128,512]{2,1,0:T(8,128)(2,1)S(1)} %pack.4), channel_id=1, source_target_pairs={{0,2},{2,4},{4,6},{6,8},{8,10},{10,12},{12,14},{14,0},{1,3},{3,5},... | collective-permute-start | bytes 786440 | tf_op jit(solution)/shard_map/ppermute | solution.py:33
  13.6 12.5 %collective-permute-start.3 = (bf16[2,128,512]{2,1,0:T(8,128)(2,1)S(1)}, bf16[2,128,512]{2,1,0:T(8,128)(2,1)S(1)}, u32[]{:S(2)}, u32[]{:S(2)}) collective-permute-start(bf16[2,128,512]{2,1,0:T(8,128)(2,1)S(1)} %pack.5), channel_id=1, source_target_pairs={{0,4},{2,6},{4,8},{6,10},{8,12},{10,14},{12,0},{14,2},{1,5},{3,7},... | collective-permute-start | bytes 786440 | tf_op jit(solution)/shard_map/ppermute | solution.py:33
  20.6 4.9 %collective-permute-start.4 = (s32[8,128]{1,0:T(8,128)S(1)}, s32[8,128]{1,0:T(8,128)S(1)}, u32[]{:S(2)}, u32[]{:S(2)}) collective-permute-start(s32[8,128]{1,0:T(8,128)S(1)} %relay.1), channel_id=1, source_target_pairs={{0,10},{2,12},{4,14},{6,0},{8,2},{10,4},{12,6},{14,8},{1,11},{3,13... | collective-permute-start | bytes 12296 | tf_op jit(solution)/shard_map/ppermute | solution.py:33

commit v3 on v2

--- a/solution.py
+++ b/solution.py
@@ -12,7 +12,7 @@
 REACH = 2
 STEPS = 2
 OFFSETS = tuple(o for o in range(-REACH, REACH + 1) if o != 0)
-PACKS = ((-2, -1), (1,), (2,))
+PACKS = ((-2, -1), (2,), (1,))
 NEAR = (-1, -2)
 ARRIVALS = ((-2, -1, 1), (2,))
 PATCH = 16

time: 27 us -> 27 us (level)
  Pallas kernels: 10.6 us -> 11.2 us
  waiting for transfers between devices: 4.18 us -> 3.61 us
    ppermute x5, waiting for transfers between devices: 4.18 us -> 3.61 us  [shifted(): lax.ppermute(block, 'grp', [(i, (i + distance) % count) for i in range(co...]
    pallas_call x1, Pallas kernels: 3.4 us -> 3.97 us  [per_device(): pl.pallas_call(stay_kernel, out_shape=[cache, heads, jax.ShapeDtypeStruct...]
  transfers between devices with their start and end apart: 5 -> 5, of which waited for: 4 -> 4; matrix products, arithmetic and copies ran while one was open for 0% -> 0% of each run, Pallas kernels for 31% -> 33%
where the time goes in v3:
time: 27 us; the launch traced here: 26.7 us
  Pallas kernels  11.2 us (41%)
  starting transfers between devices  10.6 us (39%)
  waiting for transfers between devices  3.61 us (13%)
  between operations  1.33 us (5%)
    ppermute x5, starting transfers between devices, shifted(): lax.ppermute(block, 'grp', [(i, (i + distance) % count) for i in range(co...  10.6 us
    pallas_call x3, Pallas kernels, per_device(): pl.pallas_call(functools.partial(pack_kernel, offsets), out_shape=[block]...  5.09 us
    pallas_call x1, Pallas kernels, per_device(): pl.pallas_call(stay_kernel, out_shape=[cache, heads, jax.ShapeDtypeStruct...  3.97 us
    ppermute x5, waiting for transfers between devices, shifted(): lax.ppermute(block, 'grp', [(i, (i + distance) % count) for i in range(co...  3.61 us
    pallas_call x2, Pallas kernels, per_device(): pl.pallas_call(functools.partial(arrive_kernel, mine, last), out_shape=[c...  2.1 us
  transfers between devices with their start and end apart: 5, of which 4 were waited for; matrix products, arithmetic and copies ran while one was open for 0% of the time, Pallas kernels for 33%

profile of v3, /device:TPU:0, one launch (start us, length us, event | category | flops | bytes accessed | tf_op | source)
XLA Modules:
  0.0 26.7 jit_solution(2481359409854366420)
XLA Ops:
  1.3 1.8 %pack.3 = (bf16[2,128,512]{2,1,0:T(8,128)(2,1)S(1)}, bf16[2,128,512]{2,1,0:T(8,128)(2,1)S(1)}) custom-call(s32[1]{0:T(128)S(6)} %copy.17.counts, s32[8]{0:T(128)} %hops_in.7, s32[8]{0:T(128)} %positions_in.7, bf16[8,2,128,512]{3,2,1,0:T(8,128)(2,1)} %kv.7), custom_call_target="tpu_custom_call" | custom-call | tf_op jit(solution)/shard_map/pack/pallas_call | solution.py:328
  3.0 5.1 %collective-permute-start = (bf16[2,128,512]{2,1,0:T(8,128)(2,1)S(1)}, bf16[2,128,512]{2,1,0:T(8,128)(2,1)S(1)}, u32[]{:S(2)}, u32[]{:S(2)}) collective-permute-start(bf16[2,128,512]{2,1,0:T(8,128)(2,1)S(1)} %get-tuple-element.13), channel_id=1, source_target_pairs={{0,12},{2,14},{4,0},{6,2},{8,4},{10,6},{12,8},{14,10},{1,13},{3,15... | collective-permute-start | bytes 786440 | tf_op jit(solution)/shard_map/ppermute | solution.py:33
  8.2 0.0 copy-start
  8.2 0.0 copy-start.1
  8.2 1.4 %collective-permute-start.1 = (bf16[2,128,512]{2,1,0:T(8,128)(2,1)S(1)}, bf16[2,128,512]{2,1,0:T(8,128)(2,1)S(1)}, u32[]{:S(2)}, u32[]{:S(2)}) collective-permute-start(bf16[2,128,512]{2,1,0:T(8,128)(2,1)S(1)} %get-tuple-element.14), channel_id=1, source_target_pairs={{0,14},{2,0},{4,2},{6,4},{8,6},{10,8},{12,10},{14,12},{1,15},{3,1}... | collective-permute-start | bytes 786440 | tf_op jit(solution)/shard_map/ppermute | solution.py:33
  9.5 1.7 %pack.4 = bf16[2,128,512]{2,1,0:T(8,128)(2,1)S(1)} custom-call(s32[1]{0:T(128)S(6)} %copy.17.counts, s32[8]{0:T(128)} %hops_in.7, s32[8]{0:T(128)} %positions_in.7, bf16[8,2,128,512]{3,2,1,0:T(8,128)(2,1)} %kv.7), custom_call_target="tpu_custom_call" | custom-call | tf_op jit(solution)/shard_map/pack/pallas_call | solution.py:328
  11.2 0.7 %collective-permute-start.2 = (bf16[2,128,512]{2,1,0:T(8,128)(2,1)S(1)}, bf16[2,128,512]{2,1,0:T(8,128)(2,1)S(1)}, u32[]{:S(2)}, u32[]{:S(2)}) collective-permute-start(bf16[2,128,512]{2,1,0:T(8,128)(2,1)S(1)} %pack.4), channel_id=1, source_target_pairs={{0,2},{2,4},{4,6},{6,8},{8,10},{10,12},{12,14},{14,0},{1,3},{3,5},... | collective-permute-start | bytes 786440 | tf_op jit(solution)/shard_map/ppermute | solution.py:33
  11.9 1.7 %pack.5 = bf16[2,128,512]{2,1,0:T(8,128)(2,1)S(1)} custom-call(s32[1]{0:T(128)S(6)} %copy.17.counts, s32[8]{0:T(128)} %hops_in.7, s32[8]{0:T(128)} %positions_in.7, bf16[8,2,128,512]{3,2,1,0:T(8,128)(2,1)} %kv.7), custom_call_target="tpu_custom_call" | custom-call | tf_op jit(solution)/shard_map/pack/pallas_call | solution.py:328
  13.6 1.0 %collective-permute-start.3 = (bf16[2,128,512]{2,1,0:T(8,128)(2,1)S(1)}, bf16[2,128,512]{2,1,0:T(8,128)(2,1)S(1)}, u32[]{:S(2)}, u32[]{:S(2)}) collective-permute-start(bf16[2,128,512]{2,1,0:T(8,128)(2,1)S(1)} %pack.5), channel_id=1, source_target_pairs={{0,4},{2,6},{4,8},{6,10},{8,12},{10,14},{12,0},{14,2},{1,5},{3,7},... | collective-permute-start | bytes 786440 | tf_op jit(solution)/shard_map/ppermute | solution.py:33
  14.6 0.0 copy-done
  14.6 0.0 copy-done.1
  14.6 4.0 %stay.1 = (bf16[8,2,128,512]{3,2,1,0:T(8,128)(2,1)}, bf16[8,2,4096]{2,1,0:T(2,128)(2,1)}, s32[1,128]{1,0:T(1,128)S(1)}) custom-call(s32[1]{0:T(128)S(6)} %copy.17.counts, s32[8]{0:T(128)} %hops_in.7, s32[8]{0:T(128)} %positions_in.7, bf16[8,2,128,512]{3,2,1,0:T(8,128)(2,1)} %kv.7, bf16[8,2,4096]{2,1,0:T(2,128)(2,1)S(1)} %copy-done, ...), custom_call_target="tpu_custom_call" | custom-call | flops 50000000 | bytes 4194304 | tf_op jit(solution)/shard_map/stay/pallas_call | solution.py:340
  18.6 0.0 collective-permute-done.refs_0_.refs_1_
  18.6 2.0 %collective-permute-done.1.refs_1_.refs_0_ = bf16[2,128,512]{2,1,0:T(8,128)(2,1)S(1)} collective-permute-done((bf16[2,128,512]{2,1,0:T(8,128)(2,1)S(1)}, bf16[2,128,512]{2,1,0:T(8,128)(2,1)S(1)}, u32[]{:S(2)}, u32[]{:S(2)}) %collective-permute-start.1) | collective-permute-done | bytes 262176 | tf_op jit(solution)/shard_map/ppermute | solution.py:33
  20.6 2.4 %collective-permute-start.4 = (s32[8,128]{1,0:T(8,128)S(1)}, s32[8,128]{1,0:T(8,128)S(1)}, u32[]{:S(2)}, u32[]{:S(2)}) collective-permute-start(s32[8,128]{1,0:T(8,128)S(1)} %relay.1), channel_id=1, source_target_pairs={{0,10},{2,12},{4,14},{6,0},{8,2},{10,4},{12,6},{14,8},{1,11},{3,13... | collective-permute-start | bytes 12296 | tf_op jit(solution)/shard_map/ppermute | solution.py:33
  23.0 0.3 %collective-permute-done.2.refs_2_ = bf16[2,128,512]{2,1,0:T(8,128)(2,1)S(1)} collective-permute-done((bf16[2,128,512]{2,1,0:T(8,128)(2,1)S(1)}, bf16[2,128,512]{2,1,0:T(8,128)(2,1)S(1)}, u32[]{:S(2)}, u32[]{:S(2)}) %collective-permute-start.2) | collective-permute-done | bytes 262176 | tf_op jit(solution)/shard_map/ppermute | solution.py:33
  23.3 1.5 %arrive.2 = (bf16[8,2,128,512]{3,2,1,0:T(8,128)(2,1)}, bf16[8,2,4096]{2,1,0:T(2,128)(2,1)}) custom-call(s32[1,128]{1,0:T(1,128)S(1)} %get-tuple-element.10.own, bf16[8,2,4096]{2,1,0:T(2,128)(2,1)S(1)} %copy-done, bf16[8,2,2,512]{3,2,1,0:T(2,128)(2,1)S(1)} %copy-done.1, ...), custom_call_target="tpu_custom_call", output_to_operand_aliasing={{0}: (3, {}), {1}: (4, {})} | custom-call | tf_op jit(solution)/shard_map/arrive/pallas_call | solution.py:372
  24.7 0.7 %collective-permute-done.4 = s32[8,128]{1,0:T(8,128)S(1)} collective-permute-done((s32[8,128]{1,0:T(8,128)S(1)}, s32[8,128]{1,0:T(8,128)S(1)}, u32[]{:S(2)}, u32[]{:S(2)}) %collective-permute-start.4) | collective-permute-done | bytes 4128 | tf_op jit(solution)/shard_map/ppermute | solution.py:33
  25.5 0.5 %collective-permute-done.3.refs_3_ = bf16[2,128,512]{2,1,0:T(8,128)(2,1)S(1)} collective-permute-done((bf16[2,128,512]{2,1,0:T(8,128)(2,1)S(1)}, bf16[2,128,512]{2,1,0:T(8,128)(2,1)S(1)}, u32[]{:S(2)}, u32[]{:S(2)}) %collective-permute-start.3) | collective-permute-done | bytes 262176 | tf_op jit(solution)/shard_map/ppermute | solution.py:33
  26.0 0.7 %arrive.3 = (bf16[8,2,128,512]{3,2,1,0:T(8,128)(2,1)}, bf16[8,2,4096]{2,1,0:T(2,128)(2,1)}, s32[8]{0:T(128)}) custom-call(s32[1,128]{1,0:T(1,128)S(1)} %get-tuple-element.10.own, bf16[8,2,4096]{2,1,0:T(2,128)(2,1)S(1)} %copy-done, bf16[8,2,2,512]{3,2,1,0:T(2,128)(2,1)S(1)} %copy-done.1, ...), custom_call_target="tpu_custom_call", output_to_operand_aliasing={{0}: (3, {}), {1}: (4, {})} | custom-call | tf_op jit(solution)/shard_map/arrive/pallas_call | solution.py:372
  (2 shorter events, 0.0 us)
Async XLA Ops:
  3.0 15.5 %collective-permute-start = (bf16[2,128,512]{2,1,0:T(8,128)(2,1)S(1)}, bf16[2,128,512]{2,1,0:T(8,128)(2,1)S(1)}, u32[]{:S(2)}, u32[]{:S(2)}) collective-permute-start(bf16[2,128,512]{2,1,0:T(8,128)(2,1)S(1)} %get-tuple-element.13), channel_id=1, source_target_pairs={{0,12},{2,14},{4,0},{6,2},{8,4},{10,6},{12,8},{14,10},{1,13},{3,15... | collective-permute-start | bytes 786440 | tf_op jit(solution)/shard_map/ppermute | solution.py:33
  8.2 6.4 %copy-start = (bf16[8,2,4096]{2,1,0:T(2,128)(2,1)S(1)}, bf16[8,2,4096]{2,1,0:T(2,128)(2,1)}, u32[]{:S(2)}) copy-start(bf16[8,2,4096]{2,1,0:T(2,128)(2,1)} %queries.5) | copy-start | bytes 393220
  8.2 6.4 %copy-start.1 = (bf16[8,2,2,512]{3,2,1,0:T(2,128)(2,1)S(1)}, bf16[8,2,2,512]{3,2,1,0:T(2,128)(2,1)}, u32[]{:S(2)}) copy-start(bf16[8,2,2,512]{3,2,1,0:T(2,128)(2,1)} %fresh.5) | copy-start | bytes 98308
  8.2 12.4 %collective-permute-start.1 = (bf16[2,128,512]{2,1,0:T(8,128)(2,1)S(1)}, bf16[2,128,512]{2,1,0:T(8,128)(2,1)S(1)}, u32[]{:S(2)}, u32[]{:S(2)}) collective-permute-start(bf16[2,128,512]{2,1,0:T(8,128)(2,1)S(1)} %get-tuple-element.14), channel_id=1, source_target_pairs={{0,14},{2,0},{4,2},{6,4},{8,6},{10,8},{12,10},{14,12},{1,15},{3,1}... | collective-permute-start | bytes 786440 | tf_op jit(solution)/shard_map/ppermute | solution.py:33
  11.2 12.1 %collective-permute-start.2 = (bf16[2,128,512]{2,1,0:T(8,128)(2,1)S(1)}, bf16[2,128,512]{2,1,0:T(8,128)(2,1)S(1)}, u32[]{:S(2)}, u32[]{:S(2)}) collective-permute-start(bf16[2,128,512]{2,1,0:T(8,128)(2,1)S(1)} %pack.4), channel_id=1, source_target_pairs={{0,2},{2,4},{4,6},{6,8},{8,10},{10,12},{12,14},{14,0},{1,3},{3,5},... | collective-permute-start | bytes 786440 | tf_op jit(solution)/shard_map/ppermute | solution.py:33
  13.6 12.5 %collective-permute-start.3 = (bf16[2,128,512]{2,1,0:T(8,128)(2,1)S(1)}, bf16[2,128,512]{2,1,0:T(8,128)(2,1)S(1)}, u32[]{:S(2)}, u32[]{:S(2)}) collective-permute-start(bf16[2,128,512]{2,1,0:T(8,128)(2,1)S(1)} %pack.5), channel_id=1, source_target_pairs={{0,4},{2,6},{4,8},{6,10},{8,12},{10,14},{12,0},{14,2},{1,5},{3,7},... | collective-permute-start | bytes 786440 | tf_op jit(solution)/shard_map/ppermute | solution.py:33
  20.6 4.9 %collective-permute-start.4 = (s32[8,128]{1,0:T(8,128)S(1)}, s32[8,128]{1,0:T(8,128)S(1)}, u32[]{:S(2)}, u32[]{:S(2)}) collective-permute-start(s32[8,128]{1,0:T(8,128)S(1)} %relay.1), channel_id=1, source_target_pairs={{0,10},{2,12},{4,14},{6,0},{8,2},{10,4},{12,6},{14,8},{1,11},{3,13... | collective-permute-start | bytes 12296 | tf_op jit(solution)/shard_map/ppermute | solution.py:33

commit v4 on v3

--- a/solution.py
+++ b/solution.py
@@ -12,7 +12,7 @@
 REACH = 2
 STEPS = 2
 OFFSETS = tuple(o for o in range(-REACH, REACH + 1) if o != 0)
-PACKS = ((-2, -1), (2,), (1,))
+PACKS = ((-1, -2), (2,), (1,))
 NEAR = (-1, -2)
 ARRIVALS = ((-2, -1, 1), (2,))
 PATCH = 16

time: 27 us -> 27 us (level)
  Pallas kernels: 11.2 us -> 10.6 us
  waiting for transfers between devices: 3.61 us -> 4.18 us
    ppermute x5, waiting for transfers between devices: 3.61 us -> 4.18 us  [shifted(): lax.ppermute(block, 'grp', [(i, (i + distance) % count) for i in range(co...]
    pallas_call x1, Pallas kernels: 3.97 us -> 3.4 us  [per_device(): pl.pallas_call(stay_kernel, out_shape=[cache, heads, jax.ShapeDtypeStruct...]
  transfers between devices with their start and end apart: 5 -> 5, of which waited for: 4 -> 4; matrix products, arithmetic and copies ran while one was open for 0% -> 0% of each run, Pallas kernels for 33% -> 31%
where the time goes in v4:
time: 27 us; the launch traced here: 26.7 us
  Pallas kernels  10.6 us (39%)
  starting transfers between devices  10.6 us (39%)
  waiting for transfers between devices  4.18 us (15%)
  between operations  1.33 us (5%)
    ppermute x5, starting transfers between devices, shifted(): lax.ppermute(block, 'grp', [(i, (i + distance) % count) for i in range(co...  10.6 us
    pallas_call x3, Pallas kernels, per_device(): pl.pallas_call(functools.partial(pack_kernel, offsets), out_shape=[block]...  5.09 us
    ppermute x5, waiting for transfers between devices, shifted(): lax.ppermute(block, 'grp', [(i, (i + distance) % count) for i in range(co...  4.18 us
    pallas_call x1, Pallas kernels, per_device(): pl.pallas_call(stay_kernel, out_shape=[cache, heads, jax.ShapeDtypeStruct...  3.4 us
    pallas_call x2, Pallas kernels, per_device(): pl.pallas_call(functools.partial(arrive_kernel, mine, last), out_shape=[c...  2.1 us
  transfers between devices with their start and end apart: 5, of which 4 were waited for; matrix products, arithmetic and copies ran while one was open for 0% of the time, Pallas kernels for 31%

profile of v4, /device:TPU:0, one launch (start us, length us, event | category | flops | bytes accessed | tf_op | source)
XLA Modules:
  0.0 26.7 jit_solution(15038694152676502534)
XLA Ops:
  1.3 1.8 %pack.3 = (bf16[2,128,512]{2,1,0:T(8,128)(2,1)S(1)}, bf16[2,128,512]{2,1,0:T(8,128)(2,1)S(1)}) custom-call(s32[1]{0:T(128)S(6)} %copy.17.counts, s32[8]{0:T(128)} %hops_in.7, s32[8]{0:T(128)} %positions_in.7, bf16[8,2,128,512]{3,2,1,0:T(8,128)(2,1)} %kv.7), custom_call_target="tpu_custom_call" | custom-call | tf_op jit(solution)/shard_map/pack/pallas_call | solution.py:328
  3.0 5.1 %collective-permute-start = (bf16[2,128,512]{2,1,0:T(8,128)(2,1)S(1)}, bf16[2,128,512]{2,1,0:T(8,128)(2,1)S(1)}, u32[]{:S(2)}, u32[]{:S(2)}) collective-permute-start(bf16[2,128,512]{2,1,0:T(8,128)(2,1)S(1)} %get-tuple-element.13), channel_id=1, source_target_pairs={{0,12},{2,14},{4,0},{6,2},{8,4},{10,6},{12,8},{14,10},{1,13},{3,15... | collective-permute-start | bytes 786440 | tf_op jit(solution)/shard_map/ppermute | solution.py:33
  8.2 0.0 copy-start
  8.2 0.0 copy-start.1
  8.2 1.4 %collective-permute-start.1 = (bf16[2,128,512]{2,1,0:T(8,128)(2,1)S(1)}, bf16[2,128,512]{2,1,0:T(8,128)(2,1)S(1)}, u32[]{:S(2)}, u32[]{:S(2)}) collective-permute-start(bf16[2,128,512]{2,1,0:T(8,128)(2,1)S(1)} %get-tuple-element.14), channel_id=1, source_target_pairs={{0,14},{2,0},{4,2},{6,4},{8,6},{10,8},{12,10},{14,12},{1,15},{3,1}... | collective-permute-start | bytes 786440 | tf_op jit(solution)/shard_map/ppermute | solution.py:33
  9.5 1.7 %pack.4 = bf16[2,128,512]{2,1,0:T(8,128)(2,1)S(1)} custom-call(s32[1]{0:T(128)S(6)} %copy.17.counts, s32[8]{0:T(128)} %hops_in.7, s32[8]{0:T(128)} %positions_in.7, bf16[8,2,128,512]{3,2,1,0:T(8,128)(2,1)} %kv.7), custom_call_target="tpu_custom_call" | custom-call | tf_op jit(solution)/shard_map/pack/pallas_call | solution.py:328
  11.2 0.7 %collective-permute-start.2 = (bf16[2,128,512]{2,1,0:T(8,128)(2,1)S(1)}, bf16[2,128,512]{2,1,0:T(8,128)(2,1)S(1)}, u32[]{:S(2)}, u32[]{:S(2)}) collective-permute-start(bf16[2,128,512]{2,1,0:T(8,128)(2,1)S(1)} %pack.4), channel_id=1, source_target_pairs={{0,2},{2,4},{4,6},{6,8},{8,10},{10,12},{12,14},{14,0},{1,3},{3,5},... | collective-permute-start | bytes 786440 | tf_op jit(solution)/shard_map/ppermute | solution.py:33
  11.9 1.7 %pack.5 = bf16[2,128,512]{2,1,0:T(8,128)(2,1)S(1)} custom-call(s32[1]{0:T(128)S(6)} %copy.17.counts, s32[8]{0:T(128)} %hops_in.7, s32[8]{0:T(128)} %positions_in.7, bf16[8,2,128,512]{3,2,1,0:T(8,128)(2,1)} %kv.7), custom_call_target="tpu_custom_call" | custom-call | tf_op jit(solution)/shard_map/pack/pallas_call | solution.py:328
  13.6 1.0 %collective-permute-start.3 = (bf16[2,128,512]{2,1,0:T(8,128)(2,1)S(1)}, bf16[2,128,512]{2,1,0:T(8,128)(2,1)S(1)}, u32[]{:S(2)}, u32[]{:S(2)}) collective-permute-start(bf16[2,128,512]{2,1,0:T(8,128)(2,1)S(1)} %pack.5), channel_id=1, source_target_pairs={{0,4},{2,6},{4,8},{6,10},{8,12},{10,14},{12,0},{14,2},{1,5},{3,7},... | collective-permute-start | bytes 786440 | tf_op jit(solution)/shard_map/ppermute | solution.py:33
  14.6 0.0 copy-done
  14.6 0.0 copy-done.1
  14.6 3.4 %stay.1 = (bf16[8,2,128,512]{3,2,1,0:T(8,128)(2,1)}, bf16[8,2,4096]{2,1,0:T(2,128)(2,1)}, s32[1,128]{1,0:T(1,128)S(1)}) custom-call(s32[1]{0:T(128)S(6)} %copy.17.counts, s32[8]{0:T(128)} %hops_in.7, s32[8]{0:T(128)} %positions_in.7, bf16[8,2,128,512]{3,2,1,0:T(8,128)(2,1)} %kv.7, bf16[8,2,4096]{2,1,0:T(2,128)(2,1)S(1)} %copy-done, ...), custom_call_target="tpu_custom_call" | custom-call | flops 50000000 | bytes 4194304 | tf_op jit(solution)/shard_map/stay/pallas_call | solution.py:340
  18.0 0.0 collective-permute-done.refs_0_.refs_1_
  18.0 2.6 %collective-permute-done.1.refs_1_.refs_0_ = bf16[2,128,512]{2,1,0:T(8,128)(2,1)S(1)} collective-permute-done((bf16[2,128,512]{2,1,0:T(8,128)(2,1)S(1)}, bf16[2,128,512]{2,1,0:T(8,128)(2,1)S(1)}, u32[]{:S(2)}, u32[]{:S(2)}) %collective-permute-start.1) | collective-permute-done | bytes 262176 | tf_op jit(solution)/shard_map/ppermute | solution.py:33
  20.6 2.4 %collective-permute-start.4 = (s32[8,128]{1,0:T(8,128)S(1)}, s32[8,128]{1,0:T(8,128)S(1)}, u32[]{:S(2)}, u32[]{:S(2)}) collective-permute-start(s32[8,128]{1,0:T(8,128)S(1)} %relay.1), channel_id=1, source_target_pairs={{0,10},{2,12},{4,14},{6,0},{8,2},{10,4},{12,6},{14,8},{1,11},{3,13... | collective-permute-start | bytes 12296 | tf_op jit(solution)/shard_map/ppermute | solution.py:33
  23.0 0.3 %collective-permute-done.2.refs_2_ = bf16[2,128,512]{2,1,0:T(8,128)(2,1)S(1)} collective-permute-done((bf16[2,128,512]{2,1,0:T(8,128)(2,1)S(1)}, bf16[2,128,512]{2,1,0:T(8,128)(2,1)S(1)}, u32[]{:S(2)}, u32[]{:S(2)}) %collective-permute-start.2) | collective-permute-done | bytes 262176 | tf_op jit(solution)/shard_map/ppermute | solution.py:33
  23.3 1.4 %arrive.2 = (bf16[8,2,128,512]{3,2,1,0:T(8,128)(2,1)}, bf16[8,2,4096]{2,1,0:T(2,128)(2,1)}) custom-call(s32[1,128]{1,0:T(1,128)S(1)} %get-tuple-element.10.own, bf16[8,2,4096]{2,1,0:T(2,128)(2,1)S(1)} %copy-done, bf16[8,2,2,512]{3,2,1,0:T(2,128)(2,1)S(1)} %copy-done.1, ...), custom_call_target="tpu_custom_call", output_to_operand_aliasing={{0}: (3, {}), {1}: (4, {})} | custom-call | tf_op jit(solution)/shard_map/arrive/pallas_call | solution.py:372
  24.7 0.7 %collective-permute-done.4 = s32[8,128]{1,0:T(8,128)S(1)} collective-permute-done((s32[8,128]{1,0:T(8,128)S(1)}, s32[8,128]{1,0:T(8,128)S(1)}, u32[]{:S(2)}, u32[]{:S(2)}) %collective-permute-start.4) | collective-permute-done | bytes 4128 | tf_op jit(solution)/shard_map/ppermute | solution.py:33
  25.5 0.5 %collective-permute-done.3.refs_3_ = bf16[2,128,512]{2,1,0:T(8,128)(2,1)S(1)} collective-permute-done((bf16[2,128,512]{2,1,0:T(8,128)(2,1)S(1)}, bf16[2,128,512]{2,1,0:T(8,128)(2,1)S(1)}, u32[]{:S(2)}, u32[]{:S(2)}) %collective-permute-start.3) | collective-permute-done | bytes 262176 | tf_op jit(solution)/shard_map/ppermute | solution.py:33
  26.0 0.7 %arrive.3 = (bf16[8,2,128,512]{3,2,1,0:T(8,128)(2,1)}, bf16[8,2,4096]{2,1,0:T(2,128)(2,1)}, s32[8]{0:T(128)}) custom-call(s32[1,128]{1,0:T(1,128)S(1)} %get-tuple-element.10.own, bf16[8,2,4096]{2,1,0:T(2,128)(2,1)S(1)} %copy-done, bf16[8,2,2,512]{3,2,1,0:T(2,128)(2,1)S(1)} %copy-done.1, ...), custom_call_target="tpu_custom_call", output_to_operand_aliasing={{0}: (3, {}), {1}: (4, {})} | custom-call | tf_op jit(solution)/shard_map/arrive/pallas_call | solution.py:372
  (2 shorter events, 0.0 us)
Async XLA Ops:
  3.0 14.9 %collective-permute-start = (bf16[2,128,512]{2,1,0:T(8,128)(2,1)S(1)}, bf16[2,128,512]{2,1,0:T(8,128)(2,1)S(1)}, u32[]{:S(2)}, u32[]{:S(2)}) collective-permute-start(bf16[2,128,512]{2,1,0:T(8,128)(2,1)S(1)} %get-tuple-element.13), channel_id=1, source_target_pairs={{0,12},{2,14},{4,0},{6,2},{8,4},{10,6},{12,8},{14,10},{1,13},{3,15... | collective-permute-start | bytes 786440 | tf_op jit(solution)/shard_map/ppermute | solution.py:33
  8.2 6.4 %copy-start = (bf16[8,2,4096]{2,1,0:T(2,128)(2,1)S(1)}, bf16[8,2,4096]{2,1,0:T(2,128)(2,1)}, u32[]{:S(2)}) copy-start(bf16[8,2,4096]{2,1,0:T(2,128)(2,1)} %queries.5) | copy-start | bytes 393220
  8.2 6.4 %copy-start.1 = (bf16[8,2,2,512]{3,2,1,0:T(2,128)(2,1)S(1)}, bf16[8,2,2,512]{3,2,1,0:T(2,128)(2,1)}, u32[]{:S(2)}) copy-start(bf16[8,2,2,512]{3,2,1,0:T(2,128)(2,1)} %fresh.5) | copy-start | bytes 98308
  8.2 12.4 %collective-permute-start.1 = (bf16[2,128,512]{2,1,0:T(8,128)(2,1)S(1)}, bf16[2,128,512]{2,1,0:T(8,128)(2,1)S(1)}, u32[]{:S(2)}, u32[]{:S(2)}) collective-permute-start(bf16[2,128,512]{2,1,0:T(8,128)(2,1)S(1)} %get-tuple-element.14), channel_id=1, source_target_pairs={{0,14},{2,0},{4,2},{6,4},{8,6},{10,8},{12,10},{14,12},{1,15},{3,1}... | collective-permute-start | bytes 786440 | tf_op jit(solution)/shard_map/ppermute | solution.py:33
  11.2 12.1 %collective-permute-start.2 = (bf16[2,128,512]{2,1,0:T(8,128)(2,1)S(1)}, bf16[2,128,512]{2,1,0:T(8,128)(2,1)S(1)}, u32[]{:S(2)}, u32[]{:S(2)}) collective-permute-start(bf16[2,128,512]{2,1,0:T(8,128)(2,1)S(1)} %pack.4), channel_id=1, source_target_pairs={{0,2},{2,4},{4,6},{6,8},{8,10},{10,12},{12,14},{14,0},{1,3},{3,5},... | collective-permute-start | bytes 786440 | tf_op jit(solution)/shard_map/ppermute | solution.py:33
  13.6 12.5 %collective-permute-start.3 = (bf16[2,128,512]{2,1,0:T(8,128)(2,1)S(1)}, bf16[2,128,512]{2,1,0:T(8,128)(2,1)S(1)}, u32[]{:S(2)}, u32[]{:S(2)}) collective-permute-start(bf16[2,128,512]{2,1,0:T(8,128)(2,1)S(1)} %pack.5), channel_id=1, source_target_pairs={{0,4},{2,6},{4,8},{6,10},{8,12},{10,14},{12,0},{14,2},{1,5},{3,7},... | collective-permute-start | bytes 786440 | tf_op jit(solution)/shard_map/ppermute | solution.py:33
  20.6 4.9 %collective-permute-start.4 = (s32[8,128]{1,0:T(8,128)S(1)}, s32[8,128]{1,0:T(8,128)S(1)}, u32[]{:S(2)}, u32[]{:S(2)}) collective-permute-start(s32[8,128]{1,0:T(8,128)S(1)} %relay.1), channel_id=1, source_target_pairs={{0,10},{2,12},{4,14},{6,0},{8,2},{10,4},{12,6},{14,8},{1,11},{3,13... | collective-permute-start | bytes 12296 | tf_op jit(solution)/shard_map/ppermute | solution.py:33
